TPU v7x, 32 devices: a whole 2x2x4 slice. The times are simulated.
32 devices in a mesh: dp: 8 (over y, x, core), seq: 4 (over z).
Axes of the slice: x: 2, y: 2, z: 4, core: 2. Of those that a mesh axis runs over, the one named last changes fastest.
Arguments:
- tokens: bfloat16 [8192, 2048], P(('dp', 'seq')), may hold values from -6 to 6
- queries: bfloat16 [8192, 1024], P(('dp', 'seq')), may hold values from -6 to 6
- kv_weight: bfloat16 [2048, 2048], P('seq'), may hold values from -0.0625 to 0.0625
- out_grad: bfloat16 [8192, 1024], P(('dp', 'seq')), may hold values from -6 to 6
Outputs:
- output: bfloat16 [8192, 1024], P(('dp', 'seq'))
- token_grad: bfloat16 [8192, 2048], P(('dp', 'seq'))
- query_grad: bfloat16 [8192, 1024], P(('dp', 'seq'))
- weight_grad: float32 [2048, 2048], P(('dp', 'seq'))
All inputs are finite; a program needn't handle non-finite values.
Results may differ from a plain program's by a relative error of at most 0.014.
Values may be sent and summed in bfloat16 or wider, within the bound.
A program may use at most 128 MiB of HBM per device.

v0:
```python
import math

import jax
import jax.numpy as jnp
from jax import lax
from jax.sharding import PartitionSpec as P

HEADS = 8
HD = 128


epsilon = 1e-05


def prefix(x, axis, combine, identity, reverse):
    size, place = (lax.axis_size(axis), lax.axis_index(axis))
    everything = lax.all_gather(x, axis)
    start = jnp.broadcast_to(jnp.asarray(identity, x.dtype), x.shape)

    def lap(k, before):
        at = size - 1 - k if reverse else k
        reached = at > place if reverse else at < place
        new = combine(before, everything[at])
        return jnp.where(reached, new, before)

    return lax.fori_loop(0, size, lap, start)


def feature(inputs):
    return jnp.where(inputs > 0, inputs + 1.0, jnp.exp(jnp.minimum(inputs, 0.0)))


def feature_slope(inputs):
    return jnp.where(inputs > 0, 1.0, jnp.exp(jnp.minimum(inputs, 0.0)))


def contract(formula, first_op, second_op):
    return jnp.einsum(formula, first_op, second_op, precision=lax.Precision.HIGHEST)


def add_states(earlier, latter):
    return earlier + latter


def on_device(tokens, queries, kv_weight, out_grad):
    local_rows = tokens.shape[0]
    head_width = HEADS * HD
    weights = lax.all_gather(kv_weight, "seq", axis=0, tiled=True)
    kv_local = jnp.dot(tokens, weights, preferred_element_type=jnp.float32).astype(jnp.bfloat16)
    query_f = queries.astype(jnp.float32)
    key_f = kv_local[:, :head_width].astype(jnp.float32)
    value_f = kv_local[:, head_width:].astype(jnp.float32).reshape(local_rows, HEADS, HD)
    q_feat = feature(query_f).reshape(local_rows, HEADS, HD)
    k_feat = feature(key_f).reshape(local_rows, HEADS, HD)
    positions = jnp.arange(local_rows)
    causal = (positions[:, None] >= positions[None, :]).astype(jnp.float32)[None]
    zero_state = jnp.zeros((HEADS, HD, HD), jnp.float32)
    own_state = contract("thd,the->hde", k_feat, value_f)
    before = prefix(own_state, "seq", add_states, zero_state, False)
    scores = contract("thd,shd->hts", q_feat, k_feat) * causal
    attended = contract("hts,she->the", scores, value_f) + contract("thd,hde->the", q_feat, before)
    radius = jnp.sqrt(jnp.mean(attended * attended, axis=-1, keepdims=True) + epsilon)
    normed = attended / radius
    output = normed.astype(jnp.bfloat16).reshape(local_rows, head_width)
    grad_f = out_grad.astype(jnp.float32).reshape(local_rows, HEADS, HD)
    grad_att = (grad_f - normed * jnp.mean(grad_f * normed, axis=-1, keepdims=True)) / radius
    own_grad = contract("thd,the->hde", q_feat, grad_att)
    later_sum = prefix(own_grad, "seq", add_states, zero_state, True)
    mixed_w = contract("the,she->hts", grad_att, value_f) * causal
    grad_qf = contract("hts,shd->thd", mixed_w, k_feat) + contract("the,hde->thd", grad_att, before)
    grad_kf = contract("hts,thd->shd", mixed_w, q_feat) + contract(
        "she,hde->shd", value_f, later_sum
    )
    grad_val = contract("hts,the->she", scores, grad_att) + contract(
        "shd,hde->she", k_feat, later_sum
    )
    query_grad = (grad_qf.reshape(local_rows, head_width) * feature_slope(query_f)).astype(
        jnp.bfloat16
    )
    key_grad = (grad_kf.reshape(local_rows, head_width) * feature_slope(key_f)).astype(jnp.bfloat16)
    kv_grad = jnp.concatenate(
        [key_grad, grad_val.reshape(local_rows, head_width).astype(jnp.bfloat16)], axis=1
    )
    token_grad = lax.dot_general(
        kv_grad, weights, (((1,), (1,)), ((), ())), preferred_element_type=jnp.float32
    ).astype(jnp.bfloat16)
    batch_count = lax.axis_size("dp")
    shard_count = lax.axis_size("seq")
    grad_scale = 1.0 / math.sqrt(local_rows * batch_count * shard_count)
    partial_grad = lax.psum_scatter(
        (
            lax.dot_general(
                tokens, kv_grad, (((0,), (0,)), ((), ())), preferred_element_type=jnp.float32
            )
            * grad_scale
        ).astype(jnp.bfloat16),
        "dp",
        scatter_dimension=0,
        tiled=True,
    )
    weight_grad = lax.psum_scatter(partial_grad, "seq", scatter_dimension=0, tiled=True).astype(
        jnp.float32
    )
    return (output, token_grad, query_grad, weight_grad)


def solution(mesh):
    in_specs = (
        P(("dp", "seq"), None),
        P(("dp", "seq"), None),
        P("seq", None),
        P(("dp", "seq"), None),
    )
    out_specs = (
        P(("dp", "seq"), None),
        P(("dp", "seq"), None),
        P(("dp", "seq"), None),
        P(("dp", "seq"), None),
    )
    return jax.shard_map(
        on_device, mesh=mesh, in_specs=in_specs, out_specs=out_specs, check_vma=False
    )
```

profile of v0, /device:TPU:0, one launch (start us, length us, event | category | flops | bytes accessed | tf_op | source)
XLA Modules:
  0.0 414.8 jit_solution(10534711057538429721)
XLA Ops:
  8.0 154.0 %all-gather.6.cloned.1.call-done = bf16[2048,2048]{1,0:T(8,128)(2,1)} async-done(((bf16[512,2048]{1,0:T(8,128)(2,1)}), bf16[2048,2048]{1,0:T(8,128)(2,1)}) %all-gather.6.cloned.1.call-update) | async-done | bytes 8388624 | tf_op jit(solution)/shard_map/all_gather | solution.py:48
  162.0 5.7 %convolution_convert_fusion.1 = bf16[256,2048]{1,0:T(8,128)(2,1)S(1)} fusion(bf16[256,2048]{1,0:T(8,128)(2,1)S(1)} %copy-done, bf16[2048,2048]{1,0:T(8,128)(2,1)} %all-gather.6.cloned.1.call-done), kind=kOutput, calls=%fused_computation.5 | convolution fusion | flops 2148007936 | bytes 10485760 | tf_op jit(solution)/shard_map/dot_general | solution.py:49
  170.1 1.6 copy.34
  171.7 1.4 fusion.54
  173.3 2.3 copy.38
  176.9 1.6 copy.64
  178.5 4.6 %fusion.39 = f32[8,256,256]{2,1,0:T(8,128)} fusion(f32[256,8,128]{0,2,1:T(8,128)S(1)} %bitcast.78, f32[32,8,8,128]{3,2,1,0:T(8,128)} %get-tuple-element.251), kind=kOutput, calls=%fused_computation.38 | convolution fusion | flops 805306368 | bytes 4194304 | tf_op jit(solution)/shard_map/thd,shd->hts/dot_general | solution.py:38
  183.0 34.5 %all-gather.8.cloned.1.call-done = f32[32,128,128]{2,1,0:T(8,128)} async-done(((f32[8,128,128]{2,1,0:T(8,128)}), f32[32,128,128]{2,1,0:T(8,128)}) %all-gather.8.cloned.1.call-update) | async-done | bytes 2097168 | tf_op jit(solution)/shard_map/all_gather | solution.py:17
  217.5 5.0 %while.30 = (s32[]{:T(128)}, f32[8,128,128]{2,1,0:T(8,128)S(1)}, s32[]{:T(128)}, f32[4,8,128,128]{3,2,1,0:T(8,128)}, s32[]{:T(128)}, /*index=5*/s32[]{:T(128)}) while((s32[]{:T(128)}, f32[8,128,128]{2,1,0:T(8,128)S(1)}, s32[]{:T(128)}, f32[4,8,128,128]{3,2,1,0:T(8,128)}, s32[]{:T(128)}, /*index=5*/s32[]{:T(128)}) %tuple.93), condition=%wide.region_1.2_spmd.clone, body=%wide.region_0.1_spmd.clone.sunk | while | flops 393220 | bytes 1572965 | solution.py:26
  224.3 2.6 multiply_reduce_fusion.1
  228.1 1.9 fusion.65
  230.3 3.4 fusion.52
  233.7 41.2 %all-gather.10.cloned.1.call-done = f32[32,128,128]{2,1,0:T(8,128)} async-done(((f32[8,128,128]{2,1,0:T(8,128)}), f32[32,128,128]{2,1,0:T(8,128)}) %all-gather.10.cloned.1.call-update) | async-done | bytes 2097168 | tf_op jit(solution)/shard_map/all_gather | solution.py:17
  274.9 8.0 %while.31 = (s32[]{:T(128)}, f32[8,128,128]{2,1,0:T(8,128)}, s32[]{:T(128)}, f32[4,8,128,128]{3,2,1,0:T(8,128)}, s32[]{:T(128)}, /*index=5*/s32[]{:T(128)}, s32[]{:T(128)}, s32[]{:T(128)}) while((s32[]{:T(128)}, f32[8,128,128]{2,1,0:T(8,128)}, s32[]{:T(128)}, f32[4,8,128,128]{3,2,1,0:T(8,128)}, s32[]{:T(128)}, ...), condition=%wide.region_5.6_spmd.clone, body=%wide.region_4.5_spmd.clone.sunk | while | flops 393224 | bytes 1573027 | solution.py:26
  274.9 1.9 add_select_fusion.5
  276.8 2.0 add_select_fusion.5
  278.8 2.0 add_select_fusion.5
  280.9 2.0 add_select_fusion.5
  282.9 2.6 fusion.37
  285.5 1.6 fusion.50
  287.1 2.3 fusion.24
  289.4 2.1 copy.60
  291.5 4.3 %fusion.18 = f32[8,128,256]{2,1,0:T(8,128)} fusion(f32[8,128,256]{2,1,0:T(8,128)} %fusion.50, f32[256,8,128]{0,2,1:T(8,128)S(1)} %bitcast.81, f32[8,256,256]{2,1,0:T(8,128)} %fusion.52, f32[256,256]{1,0:T(8,128)S(1)} %fusion.60), kind=kOutput, calls=%fused_computation.23 | convolution fusion | flops 806092800 | bytes 5505024 | tf_op jit(solution)/shard_map/hts,thd->shd/dot_general | solution.py:38
  295.7 2.6 copy.59
  298.4 1.5 fusion.36
  300.7 5.6 %fusion = bf16[2048,2048]{0,1:T(8,128)(2,1)} fusion(bf16[256,2048]{1,0:T(8,128)(2,1)S(1)} %copy-done, bf16[256,1024]{1,0:T(8,128)(2,1)S(1)} %copy-done.14, bf16[256,1024]{1,0:T(8,128)(2,1)S(1)} %fusion.36), kind=kOutput, calls=%fused_computation.3 | convolution fusion | flops 2157969408 | bytes 10485760 | tf_op jit(solution)/shard_map/dot_general | solution.py:92
  306.6 69.9 %reduce-scatter.5.cloned.1.call-done = bf16[256,2048]{0,1:T(8,128)(2,1)} async-done(((bf16[2048,2048]{0,1:T(8,128)(2,1)}), bf16[256,2048]{0,1:T(8,128)(2,1)}) %reduce-scatter.5.cloned.1.call-update) | async-done | bytes 1048592 | tf_op jit(solution)/shard_map/reduce_scatter | solution.py:90
  376.5 2.3 copy.62
  381.4 3.5 fusion.21
  385.3 2.2 fusion.31
  387.5 6.7 %convolution_convert_fusion = bf16[256,2048]{1,0:T(8,128)(2,1)} fusion(bf16[2048,2048]{1,0:T(8,128)(2,1)} %all-gather.6.cloned.1.call-done, bf16[256,1024]{1,0:T(8,128)(2,1)S(1)} %copy-done.15, bf16[256,1024]{1,0:T(8,128)(2,1)S(1)} %copy-done.17), kind=kOutput, calls=%fused_computation.4 | convolution fusion | flops 2150105088 | bytes 10485760 | tf_op jit(solution)/shard_map/dot_general | solution.py:84
  394.2 11.9 %reduce-scatter.7.cloned.1.call-done = bf16[64,2048]{1,0:T(8,128)(2,1)} async-done(((bf16[256,2048]{1,0:T(8,128)(2,1)}), bf16[64,2048]{1,0:T(8,128)(2,1)}) %reduce-scatter.7.cloned.1.call-update) | async-done | bytes 262160
  (66 shorter events, 19.0 us)
Async XLA Ops:
  7.2 154.8 %copy-start = (bf16[256,2048]{1,0:T(8,128)(2,1)S(1)}, bf16[256,2048]{1,0:T(8,128)(2,1)}, u32[]{:S(2)}) copy-start(bf16[256,2048]{1,0:T(8,128)(2,1)} %param.8) | copy-start | bytes 3145732
  7.2 154.8 %all-gather.6.cloned.1.call-start = ((), (), s32[]{:S(2)}) async-start(), calls=%async_computation.2 | async-start | bytes 10485760 | tf_op jit(solution)/shard_map/all_gather | solution.py:48
  7.9 209.6 %all-gather.8.cloned.1.call-start = ((), (), s32[]{:S(2)}) async-start(), calls=%async_computation.4 | async-start | bytes 2621440 | tf_op jit(solution)/shard_map/all_gather | solution.py:17
  167.7 4.0 copy-start.8
  171.7 1.5 copy-start.11
  173.2 2.4 copy-start.13
  173.2 101.7 %all-gather.10.cloned.1.call-start = ((), (), s32[]{:S(2)}) async-start(), calls=%async_computation.5 | async-start | bytes 2621440 | tf_op jit(solution)/shard_map/all_gather | solution.py:17
  222.5 4.4 %copy-start.1 = (f32[8,128,128]{2,1,0:T(8,128)}, f32[8,128,128]{2,1,0:T(8,128)S(1)}, u32[]{:S(2)}) copy-start(f32[8,128,128]{2,1,0:T(8,128)S(1)} %get-tuple-element.193) | copy-start | bytes 1572868
  222.5 1.8 copy-start.4
  224.3 2.6 copy-start.7
  230.1 146.4 %reduce-scatter.5.cloned.1.call-start = ((), (), s32[]{:S(2)}) async-start(), calls=%async_computation.3 | async-start | bytes 9437184 | tf_op jit(solution)/shard_map/reduce_scatter | solution.py:90
  282.9 2.6 copy-start.3
  282.9 2.6 copy-start.9
  282.9 4.2 %copy-start.5 = (f32[8,256,256]{2,1,0:T(8,128)S(1)}, f32[8,256,256]{2,1,0:T(8,128)}, u32[]{:S(2)}) copy-start(f32[8,256,256]{2,1,0:T(8,128)} %fusion.39) | copy-start | bytes 6291460
  295.7 2.6 copy-start.10
  298.3 2.3 copy-start.14
  299.9 0.8 copy-start.16
  306.3 72.5 %copy-start.12 = (bf16[256,8,128]{0,2,1:T(8,128)(2,1)S(1)}, bf16[256,8,128]{0,2,1:T(8,128)(2,1)}, u32[]{:S(2)}) copy-start(bf16[256,8,128]{0,2,1:T(8,128)(2,1)} %get-tuple-element.250) | copy-start | bytes 1572868
  306.3 73.5 %copy-start.2 = (f32[8,128,128]{2,1,0:T(8,128)S(1)}, f32[8,128,128]{2,1,0:T(8,128)}, u32[]{:S(2)}) copy-start(f32[8,128,128]{2,1,0:T(8,128)} %copy-done.1) | copy-start | bytes 1572868
  306.3 99.7 %reduce-scatter.7.cloned.1.call-start = ((), (), s32[]{:S(2)}) async-start(), calls=%async_computation.6 | async-start | bytes 1310720
  379.8 1.6 copy-start.6
  385.3 2.2 copy-start.15
  385.3 2.2 copy-start.17
Sparse Core Ops, SparseCore 0:
  9.6 152.3 all-gather.5
  173.3 44.1 all-gather.7
  230.2 44.6 all-gather.9
  306.4 69.9 reduce-scatter.4
  378.9 27.0 reduce-scatter.6
where the time goes:
time: 416 us; the launch traced here: 415 us
  waiting for transfers between devices  312 us (75%)
  matrix products  48.2 us (12%)
  other arithmetic  20.5 us (5%)
  local copies, waits for them, and re-layouts  19.3 us (5%)
  between operations  14.1 us (3%)
    all_gather x1, waiting for transfers between devices, on_device(): weights = lax.all_gather(kv_weight, 'seq', axis=0, tiled=True)  154 us
    all_gather x2, waiting for transfers between devices, prefix(): everything = lax.all_gather(x, axis)  75.6 us
    reduce_scatter x1, waiting for transfers between devices, on_device(): lax.psum_scatter((lax.dot_general(tokens, kv_grad, (((0,), (0,)), ((), ()...  69.9 us
    dot_general x12, matrix products, contract(): jnp.einsum(formula, first_op, second_op, precision=lax.Precision.HIGHEST)  30.2 us
    select_n x8, other arithmetic, lap(): return jnp.where(reached, new, before)  12.9 us
    unnamed x6, waiting for transfers between devices  12.6 us
    unnamed x41, local copies, waits for them, and re-layouts  8.86 us
  transfers between devices with their start and end apart: 5, of which 5 were waited for; matrix products, arithmetic and copies ran while one was open for 7% of the time, Pallas kernels for 0%

commit v1 on v0

--- a/solution.py
+++ b/solution.py
@@ -14,13 +14,13 @@
 
 def prefix(x, axis, combine, identity, reverse):
     size, place = (lax.axis_size(axis), lax.axis_index(axis))
-    everything = lax.all_gather(x, axis)
+    everything = lax.all_gather(x.astype(jnp.bfloat16), axis)
     start = jnp.broadcast_to(jnp.asarray(identity, x.dtype), x.shape)
 
     def lap(k, before):
         at = size - 1 - k if reverse else k
         reached = at > place if reverse else at < place
-        new = combine(before, everything[at])
+        new = combine(before, everything[at].astype(x.dtype))
         return jnp.where(reached, new, before)
 
     return lax.fori_loop(0, size, lap, start)
@@ -35,7 +35,12 @@
 
 
 def contract(formula, first_op, second_op):
-    return jnp.einsum(formula, first_op, second_op, precision=lax.Precision.HIGHEST)
+    return jnp.einsum(
+        formula,
+        first_op.astype(jnp.bfloat16),
+        second_op.astype(jnp.bfloat16),
+        preferred_element_type=jnp.float32,
+    )
 
 
 def add_states(earlier, latter):

time: 416 us -> 367 us (0.88)
  waiting for transfers between devices: 312 us -> 281 us
  matrix products: 48.2 us -> 35.8 us
  other arithmetic: 20.5 us -> 15.7 us
    all_gather x2, waiting for transfers between devices: 75.6 us -> 42.7 us  [prefix(): everything = lax.all_gather(x.astype(jnp.bfloat16), axis)]
    dot_general x12, matrix products: 30.2 us -> 17.8 us  [contract(): jnp.einsum(formula, first_op.astype(jnp.bfloat16), second_op.astype(jnp.b...]
    unnamed x41 -> x39, local copies, waits for them, and re-layouts: 8.86 us -> 9.38 us
where the time goes in v1:
time: 367 us; the launch traced here: 366 us
  waiting for transfers between devices  281 us (77%)
  matrix products  35.8 us (10%)
  local copies, waits for them, and re-layouts  19.2 us (5%)
  other arithmetic  15.7 us (4%)
  between operations  14 us (4%)
    all_gather x1, waiting for transfers between devices, on_device(): weights = lax.all_gather(kv_weight, 'seq', axis=0, tiled=True)  154 us
    reduce_scatter x1, waiting for transfers between devices, on_device(): lax.psum_scatter((lax.dot_general(tokens, kv_grad, (((0,), (0,)), ((), ()...  70.7 us
    all_gather x2, waiting for transfers between devices, prefix(): everything = lax.all_gather(x.astype(jnp.bfloat16), axis)  42.7 us
    dot_general x12, matrix products, contract(): jnp.einsum(formula, first_op.astype(jnp.bfloat16), second_op.astype(jnp.b...  17.8 us
    unnamed x6, waiting for transfers between devices  13.7 us
    select_n x8, other arithmetic, lap(): return jnp.where(reached, new, before)  9.93 us
    unnamed x39, local copies, waits for them, and re-layouts  9.38 us
  transfers between devices with their start and end apart: 5, of which 5 were waited for; matrix products, arithmetic and copies ran while one was open for 7% of the time, Pallas kernels for 0%

profile of v1, /device:TPU:0, one launch (start us, length us, event | category | flops | bytes accessed | tf_op | source)
XLA Modules:
  0.0 366.3 jit_solution(17375224320124260205)
XLA Ops:
  8.0 154.0 %all-gather.6.cloned.1.call-done = bf16[2048,2048]{1,0:T(8,128)(2,1)} async-done(((bf16[512,2048]{1,0:T(8,128)(2,1)}), bf16[2048,2048]{1,0:T(8,128)(2,1)}) %all-gather.6.cloned.1.call-update) | async-done | bytes 8388624 | tf_op jit(solution)/shard_map/all_gather | solution.py:53
  162.0 5.7 %convolution_convert_fusion.1 = bf16[256,2048]{1,0:T(8,128)(2,1)S(1)} fusion(bf16[256,2048]{1,0:T(8,128)(2,1)S(1)} %copy-done, bf16[2048,2048]{1,0:T(8,128)(2,1)} %all-gather.6.cloned.1.call-done), kind=kOutput, calls=%fused_computation.5 | convolution fusion | flops 2148007936 | bytes 10485760 | tf_op jit(solution)/shard_map/dot_general | solution.py:54
  169.0 1.3 copy.34
  171.4 2.3 copy.38
  175.7 2.5 fusion.17
  178.2 19.4 %all-gather.8.cloned.1.call-done = bf16[32,128,128]{2,1,0:T(8,128)(2,1)} async-done(((bf16[8,128,128]{2,1,0:T(8,128)(2,1)}), bf16[32,128,128]{2,1,0:T(8,128)(2,1)}) %all-gather.8.cloned.1.call-update) | async-done | bytes 1048592 | tf_op jit(solution)/shard_map/all_gather | solution.py:17
  197.7 5.0 %while.30 = (s32[]{:T(128)}, f32[8,128,128]{2,1,0:T(8,128)S(1)}, s32[]{:T(128)}, bf16[4,8,128,128]{3,2,1,0:T(8,128)(2,1)}, s32[]{:T(128)}, /*index=5*/s32[]{:T(128)}) while((s32[]{:T(128)}, f32[8,128,128]{2,1,0:T(8,128)S(1)}, s32[]{:T(128)}, bf16[4,8,128,128]{3,2,1,0:T(8,128)(2,1)}, s32[]{:T(128)}, /*index=5*/s32[]{:T(128)}) %tuple.93), condition=%wide.region_1.2_spmd.clone, body=%wide.region_0.1_spmd.clone.sunk | while | flops 524292 | bytes 1310821 | solution.py:26
  198.9 1.2 add_select_fusion.4
  200.2 1.2 add_select_fusion.4
  201.4 1.2 add_select_fusion.4
  202.7 1.7 multiply_reduce_fusion.1
  206.7 1.6 multiply_convert_fusion.1
  208.3 1.3 fusion.39
  209.6 1.3 fusion.38
  210.9 23.2 %all-gather.10.cloned.1.call-done = bf16[32,128,128]{2,1,0:T(8,128)(2,1)} async-done(((bf16[8,128,128]{2,1,0:T(8,128)(2,1)}), bf16[32,128,128]{2,1,0:T(8,128)(2,1)}) %all-gather.10.cloned.1.call-update) | async-done | bytes 1048592 | tf_op jit(solution)/shard_map/all_gather | solution.py:17
  234.2 5.1 %while.31 = (s32[]{:T(128)}, f32[8,128,128]{2,1,0:T(8,128)S(1)}, s32[]{:T(128)}, bf16[4,8,128,128]{3,2,1,0:T(8,128)(2,1)}, s32[]{:T(128)}, /*index=5*/s32[]{:T(128)}, s32[]{:T(128)}, s32[]{:T(128)}) while((s32[]{:T(128)}, f32[8,128,128]{2,1,0:T(8,128)S(1)}, s32[]{:T(128)}, bf16[4,8,128,128]{3,2,1,0:T(8,128)(2,1)}, s32[]{:T(128)}, ...), condition=%wide.region_5.6_spmd.clone, body=%wide.region_4.5_spmd.clone.sunk | while | flops 524296 | bytes 1310883 | solution.py:26
  234.2 1.3 add_select_fusion.5
  235.5 1.2 add_select_fusion.5
  239.3 2.4 fusion.2
  241.7 2.0 copy.60
  243.7 2.7 convolution_add_fusion.2
  246.4 2.6 copy.59
  249.0 1.5 fusion.14
  251.4 5.6 %fusion = bf16[2048,2048]{0,1:T(8,128)(2,1)} fusion(bf16[256,2048]{1,0:T(8,128)(2,1)S(1)} %copy-done, bf16[256,1024]{1,0:T(8,128)(2,1)S(1)} %copy-done.13, bf16[256,1024]{1,0:T(8,128)(2,1)S(1)} %fusion.14), kind=kOutput, calls=%fused_computation.3 | convolution fusion | flops 2157969408 | bytes 10485760 | tf_op jit(solution)/shard_map/dot_general | solution.py:97
  257.2 70.7 %reduce-scatter.5.cloned.1.call-done = bf16[256,2048]{0,1:T(8,128)(2,1)} async-done(((bf16[2048,2048]{0,1:T(8,128)(2,1)}), bf16[256,2048]{0,1:T(8,128)(2,1)}) %reduce-scatter.5.cloned.1.call-update) | async-done | bytes 1048592 | tf_op jit(solution)/shard_map/reduce_scatter | solution.py:95
  327.9 2.3 copy.62
  330.2 2.0 copy.52
  332.3 1.5 fusion.40
  334.1 1.3 copy.61
  335.4 2.5 fusion.8
  337.9 6.7 %convolution_convert_fusion = bf16[256,2048]{1,0:T(8,128)(2,1)} fusion(bf16[2048,2048]{1,0:T(8,128)(2,1)} %all-gather.6.cloned.1.call-done, bf16[256,1024]{1,0:T(8,128)(2,1)S(1)} %copy-done.14, bf16[256,1024]{1,0:T(8,128)(2,1)S(1)} %copy-done.16), kind=kOutput, calls=%fused_computation.4 | convolution fusion | flops 2150105088 | bytes 10485760 | tf_op jit(solution)/shard_map/dot_general | solution.py:89
  344.6 12.9 %reduce-scatter.7.cloned.1.call-done = bf16[64,2048]{1,0:T(8,128)(2,1)} async-done(((bf16[256,2048]{1,0:T(8,128)(2,1)}), bf16[64,2048]{1,0:T(8,128)(2,1)}) %reduce-scatter.7.cloned.1.call-update) | async-done | bytes 262160
  (64 shorter events, 14.6 us)
Async XLA Ops:
  7.2 154.8 %copy-start = (bf16[256,2048]{1,0:T(8,128)(2,1)S(1)}, bf16[256,2048]{1,0:T(8,128)(2,1)}, u32[]{:S(2)}) copy-start(bf16[256,2048]{1,0:T(8,128)(2,1)} %param.8) | copy-start | bytes 3145732
  7.2 154.8 %all-gather.6.cloned.1.call-start = ((), (), s32[]{:S(2)}) async-start(), calls=%async_computation.2 | async-start | bytes 10485760 | tf_op jit(solution)/shard_map/all_gather | solution.py:53
  7.9 189.7 %all-gather.8.cloned.1.call-start = ((), (), s32[]{:S(2)}) async-start(), calls=%async_computation.4 | async-start | bytes 1310720 | tf_op jit(solution)/shard_map/all_gather | solution.py:17
  167.7 3.6 copy-start.6
  168.0 6.2 %copy-start.8 = (bf16[32,8,8,128]{3,2,1,0:T(8,128)(2,1)}, bf16[32,8,8,128]{3,2,1,0:T(8,128)(2,1)S(1)}, u32[]{:S(2)}) copy-start(bf16[32,8,8,128]{3,2,1,0:T(8,128)(2,1)S(1)} %get-tuple-element.252) | copy-start | bytes 1572868
  170.3 1.0 copy-start.10
  171.3 2.4 copy-start.11
  171.3 62.8 %all-gather.10.cloned.1.call-start = ((), (), s32[]{:S(2)}) async-start(), calls=%async_computation.5 | async-start | bytes 1310720 | tf_op jit(solution)/shard_map/all_gather | solution.py:17
  174.7 1.0 copy-start.4
  202.7 1.7 copy-start.1
  206.6 121.3 %reduce-scatter.5.cloned.1.call-start = ((), (), s32[]{:S(2)}) async-start(), calls=%async_computation.3 | async-start | bytes 9437184 | tf_op jit(solution)/shard_map/reduce_scatter | solution.py:95
  206.7 1.6 copy-start.5
  208.3 1.3 copy-start.2
  234.2 5.1 %copy-start.9 = (bf16[32,8,8,128]{3,2,1,0:T(8,128)(2,1)S(1)}, bf16[32,8,8,128]{3,2,1,0:T(8,128)(2,1)}, u32[]{:S(2)}) copy-start(bf16[32,8,8,128]{3,2,1,0:T(8,128)(2,1)} %copy-done.8) | copy-start | bytes 1572868
  246.4 2.6 copy-start.7
  249.0 2.3 copy-start.13
  250.6 0.8 copy-start.15
  257.0 75.3 %copy-start.3 = (bf16[8,256,256]{2,1,0:T(8,128)(2,1)S(1)}, bf16[8,256,256]{2,1,0:T(8,128)(2,1)}, u32[]{:S(2)}) copy-start(bf16[8,256,256]{2,1,0:T(8,128)(2,1)} %copy-done.2) | copy-start | bytes 3145732
  257.0 100.5 %reduce-scatter.7.cloned.1.call-start = ((), (), s32[]{:S(2)}) async-start(), calls=%async_computation.6 | async-start | bytes 1310720
  334.1 1.3 copy-start.12
  334.1 3.8 %copy-start.14 = (bf16[256,1024]{1,0:T(8,128)(2,1)S(1)}, bf16[256,1024]{1,0:T(8,128)(2,1)}, u32[]{:S(2)}) copy-start(bf16[256,1024]{1,0:T(8,128)(2,1)} %copy.60) | copy-start | bytes 1572868
  335.4 2.5 copy-start.16
Sparse Core Ops, SparseCore 0:
  9.6 152.3 all-gather.5
  171.5 26.1 all-gather.7
  206.7 27.4 all-gather.9
  257.1 70.7 reduce-scatter.4
  330.4 27.1 reduce-scatter.6

commit v2 on v0

v2 whole, which is shorter than its diff:
```python
import functools
import math

import jax
import jax.numpy as jnp
from jax import lax
from jax.experimental import pallas as pl
from jax.experimental.pallas import tpu as pltpu
from jax.sharding import PartitionSpec as P

HEADS = 8
HD = 128
EPS = 1e-05
MESH = pl.DeviceIdType.MESH
BF = jnp.bfloat16
F32 = jnp.float32


def dot(a, b, ca, cb):
    return lax.dot_general(a, b, (((ca,), (cb,)), ((), ())), preferred_element_type=F32)


def feature(u):
    return jnp.where(u > 0, u + 1.0, jnp.exp(jnp.minimum(u, 0.0)))


def slope(u):
    return jnp.where(u > 0, 1.0, jnp.exp(jnp.minimum(u, 0.0)))


def bit_of(x, b):
    return (x // (1 << b)) % 2


def flip(x, mask):
    b = 0
    while mask >> b:
        if (mask >> b) & 1:
            x = x + (1 << b) * (1 - 2 * bit_of(x, b))
        b += 1
    return x


def span(bits):
    masks = [0]
    for b in bits:
        masks = masks + [m | (1 << b) for m in masks]
    return masks


def kernel(
    N, Z, S, scale,
    tok, q_ref, w_ref, og_ref,
    o_ref, tg_ref, qg_ref, wg_ref,
    wfull, kvacc, kv, kvg, tokt, ga_buf, sc_buf, mw_buf, bef_buf, fsnd, lat_buf, bsnd, owng,
    part, *rest,
):
    nb = N.bit_length() - 1
    gb = S.bit_length() - 1
    rbufs = rest[:nb]
    (fin, zbuf, loc_sem, zs_sem, zr_sem, ps_sem, pr_sem, fs_sem, fr_sem, bs_sem, br_sem,
     rs_sem, rr_sem, es_sem, er_sem) = rest[nb:]
    me = lax.axis_index("dp")
    z = lax.axis_index("seq")
    T = tok.shape[0]
    D = tok.shape[1]
    HW = HEADS * HD
    R = D // Z
    sl = me % S

    def dev(dp, zz):
        return (dp, zz)

    def up(k):
        return lax.rem(z + k, Z)

    def down(k):
        return lax.rem(z + Z - k, Z)

    barrier = pltpu.get_barrier_semaphore()
    for b in range(nb):
        pl.semaphore_signal(barrier, inc=1, device_id=dev(flip(me, 1 << b), z), device_id_type=MESH)
    for k in range(1, Z):
        pl.semaphore_signal(barrier, inc=1, device_id=dev(me, up(k)), device_id_type=MESH)
    pl.semaphore_wait(barrier, nb + Z - 1)

    def zcopy(k, p):
        return pltpu.make_async_remote_copy(
            src_ref=w_ref.at[sl, :, pl.ds(p * HW, HW)], dst_ref=wfull.at[z, p, sl],
            send_sem=zs_sem.at[k, p], recv_sem=zr_sem.at[k, p],
            device_id=dev(me, up(k)), device_id_type=MESH)

    def zland(k, p):
        o = down(k)
        return pltpu.make_async_remote_copy(
            src_ref=w_ref.at[sl, :, pl.ds(p * HW, HW)], dst_ref=wfull.at[o, p, sl],
            send_sem=zs_sem.at[k, p], recv_sem=zr_sem.at[k, p],
            device_id=dev(me, up(k)), device_id_type=MESH)

    gorder = [list(range(1, gb)) + [0], list(range(gb - 1, 0, -1)) + [0]]

    def pcopy(k, p, mask, b, landed=False):
        o = down(k)
        s_src = flip(sl, mask | (1 << b) if landed else mask)
        return pltpu.make_async_remote_copy(
            src_ref=wfull.at[o, p, s_src], dst_ref=wfull.at[o, p, s_src],
            send_sem=ps_sem.at[k, p, mask | (1 << b)], recv_sem=pr_sem.at[k, p, mask | (1 << b)],
            device_id=dev(flip(me, 1 << b), z), device_id_type=MESH)

    def mm(o, first=False):
        t = tok[:, pl.ds(pl.multiple_of(o * R, 128), R)]
        for p in range(2):
            prod = dot(t, wfull[o, p].reshape(R, HW), 1, 0)
            cols = slice(p * HW, (p + 1) * HW)
            if first:
                kvacc[:, cols] = prod
            else:
                kvacc[:, cols] += prod

    for k in range(1, Z):
        for p in range(2):
            zcopy(k, p).start()
    loc = [pltpu.make_async_copy(w_ref.at[:, :, pl.ds(p * HW, HW)], wfull.at[z, p], loc_sem.at[p]) for p in range(2)]
    for c in loc:
        c.start()
    for c0 in range(0, D, 256):
        tokt[c0:c0 + 256, :] = tok[:, c0:c0 + 256].T

    @pl.when(z == 0)
    def _():
        bef_buf[...] = jnp.zeros_like(bef_buf)

    @pl.when(z == Z - 1)
    def _():
        lat_buf[...] = jnp.zeros_like(lat_buf)

    for c in loc:
        c.wait()
    mm(z, True)
    for t in range(Z - 1 + gb):
        for j in range(gb, -1, -1):
            k = t - j + 1
            if not 1 <= k <= Z - 1:
                continue
            for p in range(2):
                bits = gorder[p]
                if j == 0:
                    zland(k, p).wait_recv()
                else:
                    for mask in span(bits[:j - 1]):
                        pcopy(k, p, mask, bits[j - 1], True).wait_recv()
                if j < gb:
                    for mask in span(bits[:j]):
                        pcopy(k, p, mask, bits[j]).start()
            if j == gb:
                mm(down(k))
    kv[...] = kvacc[...].astype(BF)

    row = lax.broadcasted_iota(jnp.int32, (T, T), 0)
    col = lax.broadcasted_iota(jnp.int32, (T, T), 1)
    causal = row >= col

    def cols_of(h):
        return (pl.ds(pl.multiple_of(h * HD, HD), HD), pl.ds(pl.multiple_of(HW + h * HD, HD), HD))

    def fcopy(h):
        return pltpu.make_async_remote_copy(
            src_ref=fsnd.at[h], dst_ref=bef_buf.at[h], send_sem=fs_sem.at[h], recv_sem=fr_sem.at[h],
            device_id=dev(me, up(1)), device_id_type=MESH)

    def bcopy(h):
        return pltpu.make_async_remote_copy(
            src_ref=bsnd.at[h], dst_ref=lat_buf.at[h], send_sem=bs_sem.at[h], recv_sem=br_sem.at[h],
            device_id=dev(me, down(1)), device_id_type=MESH)

    def forward(h, _):
        hs, vs = cols_of(h)
        kf = feature(kv[:, hs].astype(F32)).astype(BF)
        qf = feature(q_ref[:, hs].astype(F32)).astype(BF)
        v = kv[:, vs]
        own = dot(kf, v, 0, 0)

        @pl.when(z > 0)
        def _():
            fcopy(h).wait_recv()

        bef = bef_buf[h]

        @pl.when(z < Z - 1)
        def _():
            fsnd[h] = (bef.astype(F32) + own).astype(BF)
            fcopy(h).start()

        sc = jnp.where(causal, dot(qf, kf, 1, 1), 0.0).astype(BF)
        sc_buf[h] = sc
        att = dot(sc, v, 1, 0) + dot(qf, bef, 1, 0)
        rinv = lax.rsqrt(jnp.mean(att * att, axis=-1, keepdims=True) + EPS)
        normed = att * rinv
        o_ref[:, hs] = normed.astype(BF)
        g = og_ref[:, hs].astype(F32)
        ga = ((g - normed * jnp.mean(g * normed, axis=-1, keepdims=True)) * rinv).astype(BF)
        ga_buf[:, hs] = ga
        og = dot(qf, ga, 0, 0)
        owng[h] = og

        @pl.when(z == Z - 1)
        def _():
            bsnd[h] = og.astype(BF)
            bcopy(h).start()

        return 0

    lax.fori_loop(0, HEADS, forward, 0)

    order = [list(range(nb)), [0] + list(range(nb - 1, 0, -1))]

    def slot_of(mask, bits):
        s = 0
        for j, b in enumerate(bits):
            if (mask >> b) & 1:
                s += N >> (j + 1)
        return s

    def rcopy(h, p, j):
        half = N >> (j + 1)
        return pltpu.make_async_remote_copy(
            src_ref=part.at[h, p, pl.ds(half, half)], dst_ref=rbufs[j].at[h, p],
            send_sem=rs_sem.at[h, p, j], recv_sem=rr_sem.at[h, p, j],
            device_id=dev(flip(me, 1 << order[p][j]), z), device_id_type=MESH)

    def ecopy(h, k):
        return pltpu.make_async_remote_copy(
            src_ref=fin.at[h, up(k)], dst_ref=zbuf.at[h, k],
            send_sem=es_sem.at[h, k], recv_sem=er_sem.at[h, k],
            device_id=dev(me, up(k)), device_id_type=MESH)

    rd = D // N
    rb = rd // Z

    def backward(h):
        hs, vs = cols_of(h)

        @pl.when(z < Z - 1)
        def _():
            bcopy(h).wait_recv()

        lat = lat_buf[h]

        @pl.when(jnp.logical_and(z > 0, z < Z - 1))
        def _():
            bsnd[h] = (lat.astype(F32) + owng[h]).astype(BF)
            bcopy(h).start()

        key = kv[:, hs].astype(F32)
        kf = feature(key).astype(BF)
        qf = feature(q_ref[:, hs].astype(F32)).astype(BF)
        v = kv[:, vs]
        ga = ga_buf[:, hs]
        mw = jnp.where(causal, dot(ga, v, 1, 1), 0.0).astype(BF)
        mw_buf[h] = mw
        gk = dot(mw, qf, 0, 0) + dot(v, lat, 1, 1)
        gv = dot(sc_buf[h], ga, 0, 0) + dot(kf, lat, 1, 0)
        gkb = (gk * slope(key)).astype(BF)
        gvb = gv.astype(BF)
        kvg[:, hs] = gkb
        kvg[:, vs] = gvb
        chunk = jnp.concatenate([gkb, gvb], axis=1)
        for m in range(N):
            d = flip(me, m)
            res = dot(tokt[pl.ds(pl.multiple_of(d * rd, rd), rd), :], chunk, 1, 0) * scale
            res = res.reshape(Z, rb, 2 * HD).astype(BF)
            for p in range(2):
                part[h, p, slot_of(m, order[p])] = res[:, :, p * HD:(p + 1) * HD]
        for p in range(2):
            rcopy(h, p, 0).start()

    def stage(h, j):
        for p in range(2):
            half = N >> j
            rcopy(h, p, j - 1).wait_recv()
            if j < nb:
                part[h, p, 0:half] = part[h, p, 0:half] + rbufs[j - 1][h, p]
                rcopy(h, p, j).start()
            else:
                fin[h, :, p] = part[h, p, 0] + rbufs[j - 1][h, p, 0]
        if j == nb:
            for k in range(1, Z):
                ecopy(h, k).start()

    def finish(h):
        hs, vs = cols_of(h)
        total = fin[h, z].astype(F32)
        for k in range(1, Z):
            ecopy(h, k).wait_recv()
            total = total + zbuf[h, k].astype(F32)
        wg_ref[:, hs] = total[0]
        wg_ref[:, vs] = total[1]
        for k in range(1, Z):
            ecopy(h, k).wait_send()
        for p in range(2):
            for j in range(nb):
                rcopy(h, p, j).wait_send()

    def token_part(zz, _):
        w = wfull[zz]
        a = dot(kvg[:, :HW], w[0].reshape(R, HW), 1, 1)
        a = a + dot(kvg[:, HW:], w[1].reshape(R, HW), 1, 1)
        tg_ref[:, pl.ds(pl.multiple_of(zz * R, 128), R)] = a.astype(BF)
        return 0

    def query_part(h, _):
        hs, vs = cols_of(h)
        kf = feature(kv[:, hs].astype(F32)).astype(BF)
        gq = dot(mw_buf[h], kf, 1, 0) + dot(ga_buf[:, hs], bef_buf[h], 1, 1)
        qg_ref[:, hs] = (gq * slope(q_ref[:, hs].astype(F32))).astype(BF)
        return 0

    def lap(it, _):
        @pl.when(it < HEADS)
        def _():
            backward(it)

        for j in range(1, nb + 1):
            @pl.when(jnp.logical_and(it >= j, it < HEADS + j))
            def _(j=j):
                stage(it - j, j)

        @pl.when(it >= nb + 1)
        def _():
            finish(it - nb - 1)

        @pl.when(it == HEADS)
        def _():
            lax.fori_loop(0, Z, token_part, 0)

        @pl.when(it == HEADS + 1)
        def _():
            lax.fori_loop(0, HEADS, query_part, 0)

        return 0

    lax.fori_loop(0, HEADS + nb + 1, lap, 0)

    for k in range(1, Z):
        for p in range(2):
            zcopy(k, p).wait_send()
            bits = gorder[p]
            for j, b in enumerate(bits):
                for mask in span(bits[:j]):
                    pcopy(k, p, mask, b).wait_send()

    @pl.when(z < Z - 1)
    def _():
        def w(h, _):
            fcopy(h).wait_send()
            return 0
        lax.fori_loop(0, HEADS, w, 0)

    @pl.when(z > 0)
    def _():
        def w(h, _):
            bcopy(h).wait_send()
            return 0
        lax.fori_loop(0, HEADS, w, 0)


def solution(mesh):
    N = mesh.shape["dp"]
    Z = mesh.shape["seq"]

    def on_device(tokens, queries, kv_weight, out_grad):
        T, D = tokens.shape
        R = kv_weight.shape[0]
        HW = queries.shape[1]
        S = min(N, R // 16)
        r = R // S
        nb = N.bit_length() - 1
        rd = D // N
        rb = rd // Z
        scale = 1.0 / math.sqrt(T * N * Z)
        vm = pl.BlockSpec(memory_space=pltpu.VMEM)
        dma = pltpu.SemaphoreType.DMA
        scratch = [
            pltpu.VMEM((Z, 2, S, r, HW), BF),
            pltpu.VMEM((T, 2 * HW), F32),
            pltpu.VMEM((T, 2 * HW), BF),
            pltpu.VMEM((T, 2 * HW), BF),
            pltpu.VMEM((D, T), BF),
            pltpu.VMEM((T, HW), BF),
            pltpu.VMEM((HEADS, T, T), BF),
            pltpu.VMEM((HEADS, T, T), BF),
            pltpu.VMEM((HEADS, HD, HD), BF),
            pltpu.VMEM((HEADS, HD, HD), BF),
            pltpu.VMEM((HEADS, HD, HD), BF),
            pltpu.VMEM((HEADS, HD, HD), BF),
            pltpu.VMEM((HEADS, HD, HD), F32),
            pltpu.VMEM((HEADS, 2, N, Z, rb, HD), BF),
        ]
        scratch += [pltpu.VMEM((HEADS, 2, N >> (j + 1), Z, rb, HD), BF) for j in range(nb)]
        scratch += [
            pltpu.VMEM((HEADS, Z, 2, rb, HD), BF),
            pltpu.VMEM((HEADS, Z, 2, rb, HD), BF),
            dma((2,)),
            dma((Z, 2)), dma((Z, 2)),
            dma((Z, 2, S)), dma((Z, 2, S)),
            dma((HEADS,)), dma((HEADS,)),
            dma((HEADS,)), dma((HEADS,)),
            dma((HEADS, 2, nb)), dma((HEADS, 2, nb)),
            dma((HEADS, Z)), dma((HEADS, Z)),
        ]
        return pl.pallas_call(
            functools.partial(kernel, N, Z, S, scale),
            out_shape=(
                jax.ShapeDtypeStruct((T, HW), BF),
                jax.ShapeDtypeStruct((T, D), BF),
                jax.ShapeDtypeStruct((T, HW), BF),
                jax.ShapeDtypeStruct((rb, 2 * HW), F32),
            ),
            in_specs=[vm] * 4,
            out_specs=(vm,) * 4,
            scratch_shapes=scratch,
            compiler_params=pltpu.CompilerParams(
                collective_id=0, has_side_effects=True, vmem_limit_bytes=58 * 1024 * 1024
            ),
            cost_estimate=pl.CostEstimate(flops=8 * T * D * HW * 2, bytes_accessed=8 * T * D, transcendentals=T * HW * 4),
        )(tokens, queries, kv_weight.reshape(S, r, 2 * HW), out_grad)

    spec = P(("dp", "seq"), None)
    return jax.shard_map(
        on_device, mesh=mesh, in_specs=(spec, spec, P("seq", None), spec),
        out_specs=(spec,) * 4, check_vma=False,
    )
```

time: 416 us -> 129 us (0.31)
  waiting for transfers between devices: 312 us -> 0 us
  Pallas kernels: 0 us -> 123 us
  matrix products: 48.2 us -> 0 us
  other arithmetic: 20.5 us -> 0 us
  local copies, waits for them, and re-layouts: 19.3 us -> 5.85 us
  between operations: 14.1 us -> 0.66 us
    all_gather x3 -> x0, waiting for transfers between devices: 230 us -> none  [the longest x1 154 us: on_device(): weights = lax.all_gather(kv_weight, 'seq', axis=0, tiled=True)]
    pallas_call x0 -> x1, Pallas kernels: none -> 123 us  [on_device(): pl.pallas_call(functools.partial(kernel, N, Z, S, scale), out_shape=(jax....]
    reduce_scatter x1 -> x0, waiting for transfers between devices: 69.9 us -> none  [on_device(): lax.psum_scatter((lax.dot_general(tokens, kv_grad, (((0,), (0,)), ((), ()...]
    dot_general x15 -> x0, matrix products: 48.2 us -> none  [the longest x12 30.2 us: contract(): jnp.einsum(formula, first_op, second_op, precision=lax.Precision.HIGHEST)]
    select_n x9 -> x0, other arithmetic: 14.3 us -> none  [the longest x8 12.9 us: lap(): return jnp.where(reached, new, before)]
    unnamed x6 -> x0, waiting for transfers between devices: 12.6 us -> none
    reshape x5 -> x0, local copies, waits for them, and re-layouts: 8.39 us -> none  [the longest x1 2.63 us: on_device(): grad_kf.reshape(local_rows, head_width) * feature_slope(key_f)]
    unnamed x41 -> x8, local copies, waits for them, and re-layouts: 8.86 us -> 5.85 us
  transfers between devices with their start and end apart: 5 -> 0, of which waited for: 5 -> 0; matrix products, arithmetic and copies ran while one was open for 7% -> 0% of each run, Pallas kernels for 0% -> 0%
where the time goes in v2:
time: 129 us
  Pallas kernels  123 us (95%)
  local copies, waits for them, and re-layouts  5.85 us (5%)
    pallas_call x1, Pallas kernels, on_device(): pl.pallas_call(functools.partial(kernel, N, Z, S, scale), out_shape=(jax....  123 us
    unnamed x8, local copies, waits for them, and re-layouts  5.85 us

profile of v2, /device:TPU:0, one launch (start us, length us, event | category | flops | bytes accessed | tf_op | source)
XLA Modules:
  0.0 129.3 jit_solution(16155573276910711826)
XLA Ops:
  0.6 122.8 %shard_map.75 = (bf16[256,1024]{1,0:T(8,128)(2,1)}, bf16[256,2048]{1,0:T(8,128)(2,1)}, bf16[256,1024]{1,0:T(8,128)(2,1)}, f32[64,2048]{1,0:T(8,128)}) custom-call(bf16[256,2048]{1,0:T(8,128)(2,1)} %tok.1, bf16[256,1024]{1,0:T(8,128)(2,1)} %q_ref.1, bf16[8,64,2048]{2,1,0:T(8,128)(2,1)} %bitcast.1, bf16[256,1024]{1,0:T(8,128)(2,1)} %og_ref.1), custom_call_target="tpu_custom_call" | custom-call | flops 8589934592 | bytes 4194304 | tf_op jit(solution)/shard_map/pallas_call | solution.py:411
  123.4 0.0 copy-start.1
  123.4 0.0 copy-start
  123.4 2.0 %copy.12 = bf16[256,1024]{1,0:T(8,128)(2,1)} copy(bf16[256,1024]{1,0:T(8,128)(2,1)} %get-tuple-element.8) | data formatting | bytes 1048576
  125.4 2.3 %copy.13 = bf16[256,2048]{1,0:T(8,128)(2,1)} copy(bf16[256,2048]{1,0:T(8,128)(2,1)} %get-tuple-element.9) | data formatting | bytes 2097152
  127.7 0.0 copy-done.1
  127.7 0.8 copy.14
  128.5 0.0 copy-done
  128.5 0.8 copy.15
Async XLA Ops:
  123.4 4.3 %copy-start.1 = (bf16[256,1024]{1,0:T(8,128)(2,1)S(1)}, bf16[256,1024]{1,0:T(8,128)(2,1)}, u32[]{:S(2)}) copy-start(bf16[256,1024]{1,0:T(8,128)(2,1)} %get-tuple-element.10) | copy-start | bytes 1572868
  123.4 5.1 %copy-start = (f32[64,2048]{1,0:T(8,128)S(1)}, f32[64,2048]{1,0:T(8,128)}, u32[]{:S(2)}) copy-start(f32[64,2048]{1,0:T(8,128)} %get-tuple-element.11) | copy-start | bytes 1572868

commit v3 on v2

--- a/solution.py
+++ b/solution.py
@@ -10,6 +10,7 @@
 
 HEADS = 8
 HD = 128
+CHUNK = 2
 EPS = 1e-05
 MESH = pl.DeviceIdType.MESH
 BF = jnp.bfloat16
@@ -41,18 +42,11 @@
     return x
 
 
-def span(bits):
-    masks = [0]
-    for b in bits:
-        masks = masks + [m | (1 << b) for m in masks]
-    return masks
-
-
 def kernel(
     N, Z, S, scale,
     tok, q_ref, w_ref, og_ref,
     o_ref, tg_ref, qg_ref, wg_ref,
-    wfull, kvacc, kv, kvg, tokt, ga_buf, sc_buf, mw_buf, bef_buf, fsnd, lat_buf, bsnd, owng,
+    wfull, kv, kvg, tokt, ga_buf, sc_buf, mw_buf, bef_buf, fsnd, lat_buf, bsnd, owng,
     part, *rest,
 ):
     nb = N.bit_length() - 1
@@ -84,45 +78,53 @@
         pl.semaphore_signal(barrier, inc=1, device_id=dev(me, up(k)), device_id_type=MESH)
     pl.semaphore_wait(barrier, nb + Z - 1)
 
-    def zcopy(k, p):
-        return pltpu.make_async_remote_copy(
-            src_ref=w_ref.at[sl, :, pl.ds(p * HW, HW)], dst_ref=wfull.at[z, p, sl],
-            send_sem=zs_sem.at[k, p], recv_sem=zr_sem.at[k, p],
+    CW = CHUNK * HD
+    C = HEADS // CHUNK
+
+    def place(spread, flipped=None):
+        at = []
+        for b in reversed(range(gb)):
+            if b in spread:
+                at.append(slice(None))
+            else:
+                at.append(1 - bit_of(sl, b) if b == flipped else bit_of(sl, b))
+        return tuple(at)
+
+    def chunk_cols(c, p):
+        return pl.ds(pl.multiple_of(p * HW + c * CW, CW), CW)
+
+    def zcopy(c, k, p, landed=False):
+        return pltpu.make_async_remote_copy(
+            src_ref=w_ref.at[place(()) + (slice(None), chunk_cols(c, p))],
+            dst_ref=wfull.at[(c, p, down(k) if landed else z) + place(())],
+            send_sem=zs_sem.at[c, k, p], recv_sem=zr_sem.at[c, k, p],
             device_id=dev(me, up(k)), device_id_type=MESH)
 
-    def zland(k, p):
-        o = down(k)
-        return pltpu.make_async_remote_copy(
-            src_ref=w_ref.at[sl, :, pl.ds(p * HW, HW)], dst_ref=wfull.at[o, p, sl],
-            send_sem=zs_sem.at[k, p], recv_sem=zr_sem.at[k, p],
-            device_id=dev(me, up(k)), device_id_type=MESH)
-
     gorder = [list(range(1, gb)) + [0], list(range(gb - 1, 0, -1)) + [0]]
 
-    def pcopy(k, p, mask, b, landed=False):
-        o = down(k)
-        s_src = flip(sl, mask | (1 << b) if landed else mask)
-        return pltpu.make_async_remote_copy(
-            src_ref=wfull.at[o, p, s_src], dst_ref=wfull.at[o, p, s_src],
-            send_sem=ps_sem.at[k, p, mask | (1 << b)], recv_sem=pr_sem.at[k, p, mask | (1 << b)],
-            device_id=dev(flip(me, 1 << b), z), device_id_type=MESH)
-
-    def mm(o, first=False):
-        t = tok[:, pl.ds(pl.multiple_of(o * R, 128), R)]
-        for p in range(2):
-            prod = dot(t, wfull[o, p].reshape(R, HW), 1, 0)
-            cols = slice(p * HW, (p + 1) * HW)
-            if first:
-                kvacc[:, cols] = prod
-            else:
-                kvacc[:, cols] += prod
-
-    for k in range(1, Z):
-        for p in range(2):
-            zcopy(k, p).start()
-    loc = [pltpu.make_async_copy(w_ref.at[:, :, pl.ds(p * HW, HW)], wfull.at[z, p], loc_sem.at[p]) for p in range(2)]
-    for c in loc:
-        c.start()
+    def pcopy(c, k, p, j, landed=False):
+        bits = gorder[p]
+        src = wfull.at[(c, p, down(k)) + place(bits[:j])]
+        dst = wfull.at[(c, p, down(k)) + place(bits[:j], bits[j])] if landed else src
+        return pltpu.make_async_remote_copy(
+            src_ref=src, dst_ref=dst,
+            send_sem=ps_sem.at[c, k, p, j], recv_sem=pr_sem.at[c, k, p, j],
+            device_id=dev(flip(me, 1 << bits[j]), z), device_id_type=MESH)
+
+    def send_chunk(c):
+        for k in range(1, Z):
+            for p in range(2):
+                zcopy(c, k, p).start()
+
+    def loc(c, p):
+        return pltpu.make_async_copy(
+            w_ref.at[(slice(None),) * (gb + 1) + (chunk_cols(c, p),)], wfull.at[c, p, z], loc_sem.at[c, p])
+
+    for c in range(2):
+        send_chunk(c)
+    for c in range(C):
+        for p in range(2):
+            loc(c, p).start()
     for c0 in range(0, D, 256):
         tokt[c0:c0 + 256, :] = tok[:, c0:c0 + 256].T
 
@@ -134,27 +136,23 @@
     def _():
         lat_buf[...] = jnp.zeros_like(lat_buf)
 
-    for c in loc:
-        c.wait()
-    mm(z, True)
-    for t in range(Z - 1 + gb):
-        for j in range(gb, -1, -1):
-            k = t - j + 1
-            if not 1 <= k <= Z - 1:
-                continue
-            for p in range(2):
-                bits = gorder[p]
-                if j == 0:
-                    zland(k, p).wait_recv()
-                else:
-                    for mask in span(bits[:j - 1]):
-                        pcopy(k, p, mask, bits[j - 1], True).wait_recv()
-                if j < gb:
-                    for mask in span(bits[:j]):
-                        pcopy(k, p, mask, bits[j]).start()
-            if j == gb:
-                mm(down(k))
-    kv[...] = kvacc[...].astype(BF)
+    for c in range(C):
+        for p in range(2):
+            loc(c, p).wait()
+
+    def serve(c, k, j):
+        for p in range(2):
+            if j == 0:
+                zcopy(c, k, p, True).wait_recv()
+            else:
+                pcopy(c, k, p, j - 1, True).wait_recv()
+            if j < gb:
+                pcopy(c, k, p, j).start()
+
+    def project(c):
+        for p in range(2):
+            prod = dot(tok[...], wfull[c, p].reshape(D, CW), 1, 0)
+            kv[:, chunk_cols(c, p)] = prod.astype(BF)
 
     row = lax.broadcasted_iota(jnp.int32, (T, T), 0)
     col = lax.broadcasted_iota(jnp.int32, (T, T), 1)
@@ -208,9 +206,50 @@
             bsnd[h] = og.astype(BF)
             bcopy(h).start()
 
+    def pass_back(h):
+        @pl.when(z < Z - 1)
+        def _():
+            bcopy(h).wait_recv()
+
+        @pl.when(jnp.logical_and(z > 0, z < Z - 1))
+        def _():
+            bsnd[h] = (lat_buf[h].astype(F32) + owng[h]).astype(BF)
+            bcopy(h).start()
+
+    def gather_lap(it, _):
+        for k in range(1, Z):
+            if k == 1:
+                @pl.when(it + 2 < C)
+                def _():
+                    send_chunk(it + 2)
+            for j in range(gb, -1, -1):
+                dc = (k - 1 - j) // (Z - 1)
+                kk = (k - 1 - j) % (Z - 1) + 1
+                c = it + dc
+
+                @pl.when(jnp.logical_and(c >= 0, c < C))
+                def _(c=c, kk=kk, j=j):
+                    serve(c, kk, j)
+                    if j == gb and kk == Z - 1:
+                        project(c)
+                        forward(c * CHUNK, 0)
+
+            if k == 1:
+                @pl.when(it >= 2)
+                def _():
+                    def more(i, _):
+                        forward((it - 2) * CHUNK + i, 0)
+                        return 0
+                    lax.fori_loop(1, CHUNK, more, 0)
+
+        @pl.when(it >= 3)
+        def _():
+            for i in range(CHUNK):
+                pass_back((it - 3) * CHUNK + i)
+
         return 0
 
-    lax.fori_loop(0, HEADS, forward, 0)
+    lax.fori_loop(0, C + 2, gather_lap, 0)
 
     order = [list(range(nb)), [0] + list(range(nb - 1, 0, -1))]
 
@@ -240,17 +279,7 @@
     def backward(h):
         hs, vs = cols_of(h)
 
-        @pl.when(z < Z - 1)
-        def _():
-            bcopy(h).wait_recv()
-
         lat = lat_buf[h]
-
-        @pl.when(jnp.logical_and(z > 0, z < Z - 1))
-        def _():
-            bsnd[h] = (lat.astype(F32) + owng[h]).astype(BF)
-            bcopy(h).start()
-
         key = kv[:, hs].astype(F32)
         kf = feature(key).astype(BF)
         qf = feature(q_ref[:, hs].astype(F32)).astype(BF)
@@ -302,9 +331,11 @@
                 rcopy(h, p, j).wait_send()
 
     def token_part(zz, _):
-        w = wfull[zz]
-        a = dot(kvg[:, :HW], w[0].reshape(R, HW), 1, 1)
-        a = a + dot(kvg[:, HW:], w[1].reshape(R, HW), 1, 1)
+        a = jnp.zeros((T, R), F32)
+        for c in range(C):
+            for p in range(2):
+                cols = slice(p * HW + c * CW, p * HW + (c + 1) * CW)
+                a = a + dot(kvg[:, cols], wfull[c, p, zz].reshape(R, CW), 1, 1)
         tg_ref[:, pl.ds(pl.multiple_of(zz * R, 128), R)] = a.astype(BF)
         return 0
 
@@ -316,6 +347,10 @@
         return 0
 
     def lap(it, _):
+        @pl.when(it < CHUNK)
+        def _():
+            pass_back((C - 1) * CHUNK + it)
+
         @pl.when(it < HEADS)
         def _():
             backward(it)
@@ -341,13 +376,15 @@
 
     lax.fori_loop(0, HEADS + nb + 1, lap, 0)
 
-    for k in range(1, Z):
-        for p in range(2):
-            zcopy(k, p).wait_send()
-            bits = gorder[p]
-            for j, b in enumerate(bits):
-                for mask in span(bits[:j]):
-                    pcopy(k, p, mask, b).wait_send()
+    def sent(c, _):
+        for k in range(1, Z):
+            for p in range(2):
+                zcopy(c, k, p).wait_send()
+                for j in range(gb):
+                    pcopy(c, k, p, j).wait_send()
+        return 0
+
+    lax.fori_loop(0, C, sent, 0)
 
     @pl.when(z < Z - 1)
     def _():
@@ -375,14 +412,14 @@
         S = min(N, R // 16)
         r = R // S
         nb = N.bit_length() - 1
+        gb = S.bit_length() - 1
         rd = D // N
         rb = rd // Z
         scale = 1.0 / math.sqrt(T * N * Z)
         vm = pl.BlockSpec(memory_space=pltpu.VMEM)
         dma = pltpu.SemaphoreType.DMA
         scratch = [
-            pltpu.VMEM((Z, 2, S, r, HW), BF),
-            pltpu.VMEM((T, 2 * HW), F32),
+            pltpu.VMEM((HEADS // CHUNK, 2, Z) + (2,) * gb + (r, CHUNK * HD), BF),
             pltpu.VMEM((T, 2 * HW), BF),
             pltpu.VMEM((T, 2 * HW), BF),
             pltpu.VMEM((D, T), BF),
@@ -400,9 +437,9 @@
         scratch += [
             pltpu.VMEM((HEADS, Z, 2, rb, HD), BF),
             pltpu.VMEM((HEADS, Z, 2, rb, HD), BF),
-            dma((2,)),
-            dma((Z, 2)), dma((Z, 2)),
-            dma((Z, 2, S)), dma((Z, 2, S)),
+            dma((HEADS // CHUNK, 2)),
+            dma((HEADS // CHUNK, Z, 2)), dma((HEADS // CHUNK, Z, 2)),
+            dma((HEADS // CHUNK, Z, 2, gb)), dma((HEADS // CHUNK, Z, 2, gb)),
             dma((HEADS,)), dma((HEADS,)),
             dma((HEADS,)), dma((HEADS,)),
             dma((HEADS, 2, nb)), dma((HEADS, 2, nb)),
@@ -423,7 +460,7 @@
                 collective_id=0, has_side_effects=True, vmem_limit_bytes=58 * 1024 * 1024
             ),
             cost_estimate=pl.CostEstimate(flops=8 * T * D * HW * 2, bytes_accessed=8 * T * D, transcendentals=T * HW * 4),
-        )(tokens, queries, kv_weight.reshape(S, r, 2 * HW), out_grad)
+        )(tokens, queries, kv_weight.reshape((2,) * gb + (r, 2 * HW)), out_grad)
 
     spec = P(("dp", "seq"), None)
     return jax.shard_map(

time: 129 us -> 156 us (1.21)
  Pallas kernels: 123 us -> 150 us
    pallas_call x1, Pallas kernels: 123 us -> 150 us  [on_device(): pl.pallas_call(functools.partial(kernel, N, Z, S, scale), out_shape=(jax....]
where the time goes in v3:
time: 156 us
  Pallas kernels  150 us (96%)
  local copies, waits for them, and re-layouts  5.85 us (4%)
    pallas_call x1, Pallas kernels, on_device(): pl.pallas_call(functools.partial(kernel, N, Z, S, scale), out_shape=(jax....  150 us
    unnamed x8, local copies, waits for them, and re-layouts  5.85 us

profile of v3, /device:TPU:0, one launch (start us, length us, event | category | flops | bytes accessed | tf_op | source)
XLA Modules:
  0.0 156.2 jit_solution(13729605762213467800)
XLA Ops:
  0.6 149.7 %shard_map.75 = (bf16[256,1024]{1,0:T(8,128)(2,1)}, bf16[256,2048]{1,0:T(8,128)(2,1)}, bf16[256,1024]{1,0:T(8,128)(2,1)}, f32[64,2048]{1,0:T(8,128)}) custom-call(bf16[256,2048]{1,0:T(8,128)(2,1)} %tok.1, bf16[256,1024]{1,0:T(8,128)(2,1)} %q_ref.1, bf16[2,2,2,64,2048]{4,3,2,1,0:T(8,128)(2,1)} %bitcast.1, bf16[256,1024]{1,0:T(8,128)(2,1)} %og_ref.1), custom_call_target="tpu_custom_call" | custom-call | flops 8589934592 | bytes 4194304 | tf_op jit(solution)/shard_map/pallas_call | solution.py:448
  150.3 0.0 copy-start.1
  150.3 0.0 copy-start
  150.3 2.0 %copy.12 = bf16[256,1024]{1,0:T(8,128)(2,1)} copy(bf16[256,1024]{1,0:T(8,128)(2,1)} %get-tuple-element.8) | data formatting | bytes 1048576
  152.3 2.3 %copy.13 = bf16[256,2048]{1,0:T(8,128)(2,1)} copy(bf16[256,2048]{1,0:T(8,128)(2,1)} %get-tuple-element.9) | data formatting | bytes 2097152
  154.6 0.0 copy-done.1
  154.6 0.8 copy.14
  155.4 0.0 copy-done
  155.4 0.8 copy.15
Async XLA Ops:
  150.3 4.3 %copy-start.1 = (bf16[256,1024]{1,0:T(8,128)(2,1)S(1)}, bf16[256,1024]{1,0:T(8,128)(2,1)}, u32[]{:S(2)}) copy-start(bf16[256,1024]{1,0:T(8,128)(2,1)} %get-tuple-element.10) | copy-start | bytes 1572868
  150.3 5.1 %copy-start = (f32[64,2048]{1,0:T(8,128)S(1)}, f32[64,2048]{1,0:T(8,128)}, u32[]{:S(2)}) copy-start(f32[64,2048]{1,0:T(8,128)} %get-tuple-element.11) | copy-start | bytes 1572868

commit v4 on v3

--- a/solution.py
+++ b/solution.py
@@ -10,7 +10,7 @@
 
 HEADS = 8
 HD = 128
-CHUNK = 2
+CHUNK = 4
 EPS = 1e-05
 MESH = pl.DeviceIdType.MESH
 BF = jnp.bfloat16
@@ -93,34 +93,48 @@
     def chunk_cols(c, p):
         return pl.ds(pl.multiple_of(p * HW + c * CW, CW), CW)
 
-    def zcopy(c, k, p, landed=False):
+    def origin(u):
+        pairs = jnp.minimum(z, Z - 1 - z)
+        near = z - (u + 1) // 2 if u % 2 else z + u // 2
+        far = jnp.where(z > Z - 1 - z, z - (u - pairs), z + (u - pairs))
+        return jnp.where(u <= 2 * pairs, near, far)
+
+    def zcopy(c, o, p, way, own=False):
+        home = wfull.at[(c, p, o) + place(())]
+        src = w_ref.at[place(()) + (slice(None), chunk_cols(c, p))] if own else home
         return pltpu.make_async_remote_copy(
-            src_ref=w_ref.at[place(()) + (slice(None), chunk_cols(c, p))],
-            dst_ref=wfull.at[(c, p, down(k) if landed else z) + place(())],
-            send_sem=zs_sem.at[c, k, p], recv_sem=zr_sem.at[c, k, p],
-            device_id=dev(me, up(k)), device_id_type=MESH)
+            src_ref=src, dst_ref=home,
+            send_sem=zs_sem.at[c, o, p, way], recv_sem=zr_sem.at[c, o, p],
+            device_id=dev(me, down(1) if way else up(1)), device_id_type=MESH)
 
     gorder = [list(range(1, gb)) + [0], list(range(gb - 1, 0, -1)) + [0]]
 
     def pcopy(c, k, p, j, landed=False):
         bits = gorder[p]
-        src = wfull.at[(c, p, down(k)) + place(bits[:j])]
-        dst = wfull.at[(c, p, down(k)) + place(bits[:j], bits[j])] if landed else src
+        o = origin(k)
+        src = wfull.at[(c, p, o) + place(bits[:j])]
+        dst = wfull.at[(c, p, o) + place(bits[:j], bits[j])] if landed else src
         return pltpu.make_async_remote_copy(
             src_ref=src, dst_ref=dst,
             send_sem=ps_sem.at[c, k, p, j], recv_sem=pr_sem.at[c, k, p, j],
             device_id=dev(flip(me, 1 << bits[j]), z), device_id_type=MESH)
 
     def send_chunk(c):
-        for k in range(1, Z):
+        @pl.when(z < Z - 1)
+        def _():
             for p in range(2):
-                zcopy(c, k, p).start()
+                zcopy(c, z, p, 0, True).start()
+
+        @pl.when(z > 0)
+        def _():
+            for p in range(2):
+                zcopy(c, z, p, 1, True).start()
 
     def loc(c, p):
         return pltpu.make_async_copy(
             w_ref.at[(slice(None),) * (gb + 1) + (chunk_cols(c, p),)], wfull.at[c, p, z], loc_sem.at[c, p])
 
-    for c in range(2):
+    for c in range(C):
         send_chunk(c)
     for c in range(C):
         for p in range(2):
@@ -143,7 +157,16 @@
     def serve(c, k, j):
         for p in range(2):
             if j == 0:
-                zcopy(c, k, p, True).wait_recv()
+                o = origin(k)
+                zcopy(c, o, p, 0).wait_recv()
+
+                @pl.when(jnp.logical_and(o < z, z < Z - 1))
+                def _(o=o, p=p):
+                    zcopy(c, o, p, 0).start()
+
+                @pl.when(jnp.logical_and(o > z, z > 0))
+                def _(o=o, p=p):
+                    zcopy(c, o, p, 1).start()
             else:
                 pcopy(c, k, p, j - 1, True).wait_recv()
             if j < gb:
@@ -218,10 +241,7 @@
 
     def gather_lap(it, _):
         for k in range(1, Z):
-            if k == 1:
-                @pl.when(it + 2 < C)
-                def _():
-                    send_chunk(it + 2)
+            done = None
             for j in range(gb, -1, -1):
                 dc = (k - 1 - j) // (Z - 1)
                 kk = (k - 1 - j) % (Z - 1) + 1
@@ -230,22 +250,30 @@
                 @pl.when(jnp.logical_and(c >= 0, c < C))
                 def _(c=c, kk=kk, j=j):
                     serve(c, kk, j)
-                    if j == gb and kk == Z - 1:
-                        project(c)
-                        forward(c * CHUNK, 0)
-
-            if k == 1:
-                @pl.when(it >= 2)
-                def _():
-                    def more(i, _):
-                        forward((it - 2) * CHUNK + i, 0)
-                        return 0
-                    lax.fori_loop(1, CHUNK, more, 0)
+
+                if j == gb and kk == Z - 1:
+                    done = c
+            heads = range(k, CHUNK if k == Z - 1 else min(k + 1, CHUNK))
+
+            @pl.when(it >= 2)
+            def _(heads=heads):
+                for i in heads:
+                    forward((it - 2) * CHUNK + i, 0)
+
+            @pl.when(it >= 3)
+            def _(heads=heads):
+                for i in heads:
+                    pass_back((it - 3) * CHUNK + i - 1)
+
+            if done is not None:
+                @pl.when(jnp.logical_and(done >= 0, done < C))
+                def _(c=done):
+                    project(c)
+                    forward(c * CHUNK, 0)
 
         @pl.when(it >= 3)
         def _():
-            for i in range(CHUNK):
-                pass_back((it - 3) * CHUNK + i)
+            pass_back((it - 3) * CHUNK + CHUNK - 1)
 
         return 0
 
@@ -377,9 +405,26 @@
     lax.fori_loop(0, HEADS + nb + 1, lap, 0)
 
     def sent(c, _):
-        for k in range(1, Z):
-            for p in range(2):
-                zcopy(c, k, p).wait_send()
+        for p in range(2):
+            @pl.when(z < Z - 1)
+            def _(p=p):
+                zcopy(c, z, p, 0, True).wait_send()
+
+            @pl.when(z > 0)
+            def _(p=p):
+                zcopy(c, z, p, 1, True).wait_send()
+
+            for k in range(1, Z):
+                o = origin(k)
+
+                @pl.when(jnp.logical_and(o < z, z < Z - 1))
+                def _(o=o, p=p):
+                    zcopy(c, o, p, 0).wait_send()
+
+                @pl.when(jnp.logical_and(o > z, z > 0))
+                def _(o=o, p=p):
+                    zcopy(c, o, p, 1).wait_send()
+
                 for j in range(gb):
                     pcopy(c, k, p, j).wait_send()
         return 0
@@ -438,7 +483,7 @@
             pltpu.VMEM((HEADS, Z, 2, rb, HD), BF),
             pltpu.VMEM((HEADS, Z, 2, rb, HD), BF),
             dma((HEADS // CHUNK, 2)),
-            dma((HEADS // CHUNK, Z, 2)), dma((HEADS // CHUNK, Z, 2)),
+            dma((HEADS // CHUNK, Z, 2, 2)), dma((HEADS // CHUNK, Z, 2)),
             dma((HEADS // CHUNK, Z, 2, gb)), dma((HEADS // CHUNK, Z, 2, gb)),
             dma((HEADS,)), dma((HEADS,)),
             dma((HEADS,)), dma((HEADS,)),

time: 156 us -> 153 us (0.981)
  Pallas kernels: 150 us -> 146 us
    pallas_call x1, Pallas kernels: 150 us -> 146 us  [on_device(): pl.pallas_call(functools.partial(kernel, N, Z, S, scale), out_shape=(jax....]
where the time goes in v4:
time: 153 us
  Pallas kernels  146 us (95%)
  local copies, waits for them, and re-layouts  5.85 us (4%)
    pallas_call x1, Pallas kernels, on_device(): pl.pallas_call(functools.partial(kernel, N, Z, S, scale), out_shape=(jax....  146 us
    unnamed x8, local copies, waits for them, and re-layouts  5.85 us

profile of v4, /device:TPU:0, one launch (start us, length us, event | category | flops | bytes accessed | tf_op | source)
XLA Modules:
  0.0 152.7 jit_solution(14773517575696690903)
XLA Ops:
  0.6 146.2 %shard_map.75 = (bf16[256,1024]{1,0:T(8,128)(2,1)}, bf16[256,2048]{1,0:T(8,128)(2,1)}, bf16[256,1024]{1,0:T(8,128)(2,1)}, f32[64,2048]{1,0:T(8,128)}) custom-call(bf16[256,2048]{1,0:T(8,128)(2,1)} %tok.1, bf16[256,1024]{1,0:T(8,128)(2,1)} %q_ref.1, bf16[2,2,2,64,2048]{4,3,2,1,0:T(8,128)(2,1)} %bitcast.1, bf16[256,1024]{1,0:T(8,128)(2,1)} %og_ref.1), custom_call_target="tpu_custom_call" | custom-call | flops 8589934592 | bytes 4194304 | tf_op jit(solution)/shard_map/pallas_call | solution.py:493
  146.9 0.0 copy-start.1
  146.9 0.0 copy-start
  146.9 2.0 %copy.12 = bf16[256,1024]{1,0:T(8,128)(2,1)} copy(bf16[256,1024]{1,0:T(8,128)(2,1)} %get-tuple-element.8) | data formatting | bytes 1048576
  148.8 2.3 %copy.13 = bf16[256,2048]{1,0:T(8,128)(2,1)} copy(bf16[256,2048]{1,0:T(8,128)(2,1)} %get-tuple-element.9) | data formatting | bytes 2097152
  151.1 0.0 copy-done.1
  151.1 0.8 copy.14
  151.9 0.0 copy-done
  151.9 0.8 copy.15
Async XLA Ops:
  146.9 4.3 %copy-start.1 = (bf16[256,1024]{1,0:T(8,128)(2,1)S(1)}, bf16[256,1024]{1,0:T(8,128)(2,1)}, u32[]{:S(2)}) copy-start(bf16[256,1024]{1,0:T(8,128)(2,1)} %get-tuple-element.10) | copy-start | bytes 1572868
  146.9 5.1 %copy-start = (f32[64,2048]{1,0:T(8,128)S(1)}, f32[64,2048]{1,0:T(8,128)}, u32[]{:S(2)}) copy-start(f32[64,2048]{1,0:T(8,128)} %get-tuple-element.11) | copy-start | bytes 1572868

commit v5 on v2

--- a/solution.py
+++ b/solution.py
@@ -10,6 +10,7 @@
 
 HEADS = 8
 HD = 128
+LAG = 4
 EPS = 1e-05
 MESH = pl.DeviceIdType.MESH
 BF = jnp.bfloat16
@@ -84,23 +85,37 @@
         pl.semaphore_signal(barrier, inc=1, device_id=dev(me, up(k)), device_id_type=MESH)
     pl.semaphore_wait(barrier, nb + Z - 1)
 
-    def zcopy(k, p):
-        return pltpu.make_async_remote_copy(
-            src_ref=w_ref.at[sl, :, pl.ds(p * HW, HW)], dst_ref=wfull.at[z, p, sl],
-            send_sem=zs_sem.at[k, p], recv_sem=zr_sem.at[k, p],
-            device_id=dev(me, up(k)), device_id_type=MESH)
-
-    def zland(k, p):
-        o = down(k)
-        return pltpu.make_async_remote_copy(
-            src_ref=w_ref.at[sl, :, pl.ds(p * HW, HW)], dst_ref=wfull.at[o, p, sl],
-            send_sem=zs_sem.at[k, p], recv_sem=zr_sem.at[k, p],
-            device_id=dev(me, up(k)), device_id_type=MESH)
+    def origin(u):
+        pairs = jnp.minimum(z, Z - 1 - z)
+        near = z - (u + 1) // 2 if u % 2 else z + u // 2
+        far = jnp.where(z > Z - 1 - z, z - (u - pairs), z + (u - pairs))
+        return jnp.where(u <= 2 * pairs, near, far)
+
+    def zcopy(o, p, way, own=False):
+        home = wfull.at[o, p, sl]
+        return pltpu.make_async_remote_copy(
+            src_ref=w_ref.at[sl, :, pl.ds(p * HW, HW)] if own else home, dst_ref=home,
+            send_sem=zs_sem.at[o, p, way], recv_sem=zr_sem.at[o, p],
+            device_id=dev(me, down(1) if way else up(1)), device_id_type=MESH)
+
+    def relay(o, p, wait):
+        for way, cond in enumerate((jnp.logical_and(o < z, z < Z - 1), jnp.logical_and(o > z, z > 0))):
+            @pl.when(cond)
+            def _(way=way):
+                c = zcopy(o, p, way)
+                c.wait_send() if wait else c.start()
+
+    def offer(p, wait):
+        for way, cond in enumerate((z < Z - 1, z > 0)):
+            @pl.when(cond)
+            def _(way=way):
+                c = zcopy(z, p, way, True)
+                c.wait_send() if wait else c.start()
 
     gorder = [list(range(1, gb)) + [0], list(range(gb - 1, 0, -1)) + [0]]
 
     def pcopy(k, p, mask, b, landed=False):
-        o = down(k)
+        o = origin(k)
         s_src = flip(sl, mask | (1 << b) if landed else mask)
         return pltpu.make_async_remote_copy(
             src_ref=wfull.at[o, p, s_src], dst_ref=wfull.at[o, p, s_src],
@@ -117,9 +132,8 @@
             else:
                 kvacc[:, cols] += prod
 
-    for k in range(1, Z):
-        for p in range(2):
-            zcopy(k, p).start()
+    for p in range(2):
+        offer(p, False)
     loc = [pltpu.make_async_copy(w_ref.at[:, :, pl.ds(p * HW, HW)], wfull.at[z, p], loc_sem.at[p]) for p in range(2)]
     for c in loc:
         c.start()
@@ -145,7 +159,8 @@
             for p in range(2):
                 bits = gorder[p]
                 if j == 0:
-                    zland(k, p).wait_recv()
+                    zcopy(origin(k), p, 0).wait_recv()
+                    relay(origin(k), p, False)
                 else:
                     for mask in span(bits[:j - 1]):
                         pcopy(k, p, mask, bits[j - 1], True).wait_recv()
@@ -153,7 +168,7 @@
                     for mask in span(bits[:j]):
                         pcopy(k, p, mask, bits[j]).start()
             if j == gb:
-                mm(down(k))
+                mm(origin(k))
     kv[...] = kvacc[...].astype(BF)
 
     row = lax.broadcasted_iota(jnp.int32, (T, T), 0)
@@ -208,7 +223,21 @@
             bsnd[h] = og.astype(BF)
             bcopy(h).start()
 
+        @pl.when(h >= LAG)
+        def _():
+            pass_back(h - LAG)
+
         return 0
+
+    def pass_back(h):
+        @pl.when(z < Z - 1)
+        def _():
+            bcopy(h).wait_recv()
+
+        @pl.when(jnp.logical_and(z > 0, z < Z - 1))
+        def _():
+            bsnd[h] = (lat_buf[h].astype(F32) + owng[h]).astype(BF)
+            bcopy(h).start()
 
     lax.fori_loop(0, HEADS, forward, 0)
 
@@ -240,17 +269,7 @@
     def backward(h):
         hs, vs = cols_of(h)
 
-        @pl.when(z < Z - 1)
-        def _():
-            bcopy(h).wait_recv()
-
         lat = lat_buf[h]
-
-        @pl.when(jnp.logical_and(z > 0, z < Z - 1))
-        def _():
-            bsnd[h] = (lat.astype(F32) + owng[h]).astype(BF)
-            bcopy(h).start()
-
         key = kv[:, hs].astype(F32)
         kf = feature(key).astype(BF)
         qf = feature(q_ref[:, hs].astype(F32)).astype(BF)
@@ -316,6 +335,10 @@
         return 0
 
     def lap(it, _):
+        @pl.when(it < LAG)
+        def _():
+            pass_back(HEADS - LAG + it)
+
         @pl.when(it < HEADS)
         def _():
             backward(it)
@@ -341,9 +364,11 @@
 
     lax.fori_loop(0, HEADS + nb + 1, lap, 0)
 
+    for p in range(2):
+        offer(p, True)
     for k in range(1, Z):
         for p in range(2):
-            zcopy(k, p).wait_send()
+            relay(origin(k), p, True)
             bits = gorder[p]
             for j, b in enumerate(bits):
                 for mask in span(bits[:j]):
@@ -401,7 +426,7 @@
             pltpu.VMEM((HEADS, Z, 2, rb, HD), BF),
             pltpu.VMEM((HEADS, Z, 2, rb, HD), BF),
             dma((2,)),
-            dma((Z, 2)), dma((Z, 2)),
+            dma((Z, 2, 2)), dma((Z, 2)),
             dma((Z, 2, S)), dma((Z, 2, S)),
             dma((HEADS,)), dma((HEADS,)),
             dma((HEADS,)), dma((HEADS,)),

time: 129 us -> 158 us (1.22)
  Pallas kernels: 123 us -> 152 us
    pallas_call x1, Pallas kernels: 123 us -> 152 us  [on_device(): pl.pallas_call(functools.partial(kernel, N, Z, S, scale), out_shape=(jax....]
where the time goes in v5:
time: 158 us
  Pallas kernels  152 us (96%)
  local copies, waits for them, and re-layouts  5.85 us (4%)
    pallas_call x1, Pallas kernels, on_device(): pl.pallas_call(functools.partial(kernel, N, Z, S, scale), out_shape=(jax....  152 us
    unnamed x8, local copies, waits for them, and re-layouts  5.85 us

profile of v5, /device:TPU:0, one launch (start us, length us, event | category | flops | bytes accessed | tf_op | source)
XLA Modules:
  0.0 158.1 jit_solution(13574472981083865451)
XLA Ops:
  0.6 151.6 %shard_map.75 = (bf16[256,1024]{1,0:T(8,128)(2,1)}, bf16[256,2048]{1,0:T(8,128)(2,1)}, bf16[256,1024]{1,0:T(8,128)(2,1)}, f32[64,2048]{1,0:T(8,128)}) custom-call(bf16[256,2048]{1,0:T(8,128)(2,1)} %tok.1, bf16[256,1024]{1,0:T(8,128)(2,1)} %q_ref.1, bf16[8,64,2048]{2,1,0:T(8,128)(2,1)} %bitcast.1, bf16[256,1024]{1,0:T(8,128)(2,1)} %og_ref.1), custom_call_target="tpu_custom_call" | custom-call | flops 8589934592 | bytes 4194304 | tf_op jit(solution)/shard_map/pallas_call | solution.py:436
  152.2 0.0 copy-start.1
  152.2 0.0 copy-start
  152.2 2.0 %copy.12 = bf16[256,1024]{1,0:T(8,128)(2,1)} copy(bf16[256,1024]{1,0:T(8,128)(2,1)} %get-tuple-element.8) | data formatting | bytes 1048576
  154.2 2.3 %copy.13 = bf16[256,2048]{1,0:T(8,128)(2,1)} copy(bf16[256,2048]{1,0:T(8,128)(2,1)} %get-tuple-element.9) | data formatting | bytes 2097152
  156.5 0.0 copy-done.1
  156.5 0.8 copy.14
  157.3 0.0 copy-done
  157.3 0.8 copy.15
Async XLA Ops:
  152.2 4.3 %copy-start.1 = (bf16[256,1024]{1,0:T(8,128)(2,1)S(1)}, bf16[256,1024]{1,0:T(8,128)(2,1)}, u32[]{:S(2)}) copy-start(bf16[256,1024]{1,0:T(8,128)(2,1)} %get-tuple-element.10) | copy-start | bytes 1572868
  152.2 5.1 %copy-start = (f32[64,2048]{1,0:T(8,128)S(1)}, f32[64,2048]{1,0:T(8,128)}, u32[]{:S(2)}) copy-start(f32[64,2048]{1,0:T(8,128)} %get-tuple-element.11) | copy-start | bytes 1572868

commit v6 on v4

--- a/solution.py
+++ b/solution.py
@@ -260,20 +260,11 @@
                 for i in heads:
                     forward((it - 2) * CHUNK + i, 0)
 
-            @pl.when(it >= 3)
-            def _(heads=heads):
-                for i in heads:
-                    pass_back((it - 3) * CHUNK + i - 1)
-
             if done is not None:
                 @pl.when(jnp.logical_and(done >= 0, done < C))
                 def _(c=done):
                     project(c)
                     forward(c * CHUNK, 0)
-
-        @pl.when(it >= 3)
-        def _():
-            pass_back((it - 3) * CHUNK + CHUNK - 1)
 
         return 0
 
@@ -375,12 +366,9 @@
         return 0
 
     def lap(it, _):
-        @pl.when(it < CHUNK)
-        def _():
-            pass_back((C - 1) * CHUNK + it)
-
         @pl.when(it < HEADS)
         def _():
+            pass_back(it)
             backward(it)
 
         for j in range(1, nb + 1):

time: 153 us -> 135 us (0.88)
  Pallas kernels: 146 us -> 128 us
    pallas_call x1, Pallas kernels: 146 us -> 128 us  [on_device(): pl.pallas_call(functools.partial(kernel, N, Z, S, scale), out_shape=(jax....]
where the time goes in v6:
time: 135 us
  Pallas kernels  128 us (95%)
  local copies, waits for them, and re-layouts  5.85 us (4%)
    pallas_call x1, Pallas kernels, on_device(): pl.pallas_call(functools.partial(kernel, N, Z, S, scale), out_shape=(jax....  128 us
    unnamed x8, local copies, waits for them, and re-layouts  5.85 us

profile of v6, /device:TPU:0, one launch (start us, length us, event | category | flops | bytes accessed | tf_op | source)
XLA Modules:
  0.0 134.8 jit_solution(12014049011397721402)
XLA Ops:
  0.6 128.3 %shard_map.75 = (bf16[256,1024]{1,0:T(8,128)(2,1)}, bf16[256,2048]{1,0:T(8,128)(2,1)}, bf16[256,1024]{1,0:T(8,128)(2,1)}, f32[64,2048]{1,0:T(8,128)}) custom-call(bf16[256,2048]{1,0:T(8,128)(2,1)} %tok.1, bf16[256,1024]{1,0:T(8,128)(2,1)} %q_ref.1, bf16[2,2,2,64,2048]{4,3,2,1,0:T(8,128)(2,1)} %bitcast.1, bf16[256,1024]{1,0:T(8,128)(2,1)} %og_ref.1), custom_call_target="tpu_custom_call" | custom-call | flops 8589934592 | bytes 4194304 | tf_op jit(solution)/shard_map/pallas_call | solution.py:481
  128.9 0.0 copy-start.1
  128.9 0.0 copy-start
  128.9 2.0 %copy.12 = bf16[256,1024]{1,0:T(8,128)(2,1)} copy(bf16[256,1024]{1,0:T(8,128)(2,1)} %get-tuple-element.8) | data formatting | bytes 1048576
  130.9 2.3 %copy.13 = bf16[256,2048]{1,0:T(8,128)(2,1)} copy(bf16[256,2048]{1,0:T(8,128)(2,1)} %get-tuple-element.9) | data formatting | bytes 2097152
  133.2 0.0 copy-done.1
  133.2 0.8 copy.14
  134.0 0.0 copy-done
  134.0 0.8 copy.15
Async XLA Ops:
  128.9 4.3 %copy-start.1 = (bf16[256,1024]{1,0:T(8,128)(2,1)S(1)}, bf16[256,1024]{1,0:T(8,128)(2,1)}, u32[]{:S(2)}) copy-start(bf16[256,1024]{1,0:T(8,128)(2,1)} %get-tuple-element.10) | copy-start | bytes 1572868
  128.9 5.1 %copy-start = (f32[64,2048]{1,0:T(8,128)S(1)}, f32[64,2048]{1,0:T(8,128)}, u32[]{:S(2)}) copy-start(f32[64,2048]{1,0:T(8,128)} %get-tuple-element.11) | copy-start | bytes 1572868

commit v7 on v2

--- a/solution.py
+++ b/solution.py
@@ -10,6 +10,7 @@
 
 HEADS = 8
 HD = 128
+PAIR = 2
 EPS = 1e-05
 MESH = pl.DeviceIdType.MESH
 BF = jnp.bfloat16
@@ -84,23 +85,23 @@
         pl.semaphore_signal(barrier, inc=1, device_id=dev(me, up(k)), device_id_type=MESH)
     pl.semaphore_wait(barrier, nb + Z - 1)
 
-    def zcopy(k, p):
-        return pltpu.make_async_remote_copy(
-            src_ref=w_ref.at[sl, :, pl.ds(p * HW, HW)], dst_ref=wfull.at[z, p, sl],
-            send_sem=zs_sem.at[k, p], recv_sem=zr_sem.at[k, p],
-            device_id=dev(me, up(k)), device_id_type=MESH)
-
-    def zland(k, p):
-        o = down(k)
+    def origin(u):
+        pairs = jnp.minimum(z, Z - 1 - z)
+        near = z - (u + 1) // 2 if u % 2 else z + u // 2
+        far = jnp.where(z > Z - 1 - z, z - (u - pairs), z + (u - pairs))
+        return jnp.where(u <= 2 * pairs, near, far)
+
+    def zcopy(u, p, landed=False):
+        o = origin(u) if landed else z
         return pltpu.make_async_remote_copy(
             src_ref=w_ref.at[sl, :, pl.ds(p * HW, HW)], dst_ref=wfull.at[o, p, sl],
-            send_sem=zs_sem.at[k, p], recv_sem=zr_sem.at[k, p],
-            device_id=dev(me, up(k)), device_id_type=MESH)
+            send_sem=zs_sem.at[u, p], recv_sem=zr_sem.at[o, p],
+            device_id=dev(me, origin(u)), device_id_type=MESH)
 
     gorder = [list(range(1, gb)) + [0], list(range(gb - 1, 0, -1)) + [0]]
 
     def pcopy(k, p, mask, b, landed=False):
-        o = down(k)
+        o = origin(k)
         s_src = flip(sl, mask | (1 << b) if landed else mask)
         return pltpu.make_async_remote_copy(
             src_ref=wfull.at[o, p, s_src], dst_ref=wfull.at[o, p, s_src],
@@ -145,7 +146,7 @@
             for p in range(2):
                 bits = gorder[p]
                 if j == 0:
-                    zland(k, p).wait_recv()
+                    zcopy(k, p, True).wait_recv()
                 else:
                     for mask in span(bits[:j - 1]):
                         pcopy(k, p, mask, bits[j - 1], True).wait_recv()
@@ -153,7 +154,7 @@
                     for mask in span(bits[:j]):
                         pcopy(k, p, mask, bits[j]).start()
             if j == gb:
-                mm(down(k))
+                mm(origin(k))
     kv[...] = kvacc[...].astype(BF)
 
     row = lax.broadcasted_iota(jnp.int32, (T, T), 0)
@@ -173,44 +174,51 @@
             src_ref=bsnd.at[h], dst_ref=lat_buf.at[h], send_sem=bs_sem.at[h], recv_sem=br_sem.at[h],
             device_id=dev(me, down(1)), device_id_type=MESH)
 
-    def forward(h, _):
-        hs, vs = cols_of(h)
-        kf = feature(kv[:, hs].astype(F32)).astype(BF)
-        qf = feature(q_ref[:, hs].astype(F32)).astype(BF)
-        v = kv[:, vs]
-        own = dot(kf, v, 0, 0)
+    def forward(i, _):
+        heads = [i * PAIR + n for n in range(PAIR)]
+        kfs, qfs, vs_, owns = [], [], [], []
+        for h in heads:
+            hs, vs = cols_of(h)
+            kf = feature(kv[:, hs].astype(F32)).astype(BF)
+            v = kv[:, vs]
+            kfs.append(kf)
+            qfs.append(feature(q_ref[:, hs].astype(F32)).astype(BF))
+            vs_.append(v)
+            owns.append(dot(kf, v, 0, 0))
 
         @pl.when(z > 0)
         def _():
-            fcopy(h).wait_recv()
-
-        bef = bef_buf[h]
+            for h in heads:
+                fcopy(h).wait_recv()
 
         @pl.when(z < Z - 1)
         def _():
-            fsnd[h] = (bef.astype(F32) + own).astype(BF)
-            fcopy(h).start()
-
-        sc = jnp.where(causal, dot(qf, kf, 1, 1), 0.0).astype(BF)
-        sc_buf[h] = sc
-        att = dot(sc, v, 1, 0) + dot(qf, bef, 1, 0)
-        rinv = lax.rsqrt(jnp.mean(att * att, axis=-1, keepdims=True) + EPS)
-        normed = att * rinv
-        o_ref[:, hs] = normed.astype(BF)
-        g = og_ref[:, hs].astype(F32)
-        ga = ((g - normed * jnp.mean(g * normed, axis=-1, keepdims=True)) * rinv).astype(BF)
-        ga_buf[:, hs] = ga
-        og = dot(qf, ga, 0, 0)
-        owng[h] = og
+            for h, own in zip(heads, owns):
+                fsnd[h] = (bef_buf[h].astype(F32) + own).astype(BF)
+                fcopy(h).start()
+
+        scs = [jnp.where(causal, dot(qf, kf, 1, 1), 0.0).astype(BF) for qf, kf in zip(qfs, kfs)]
+        atts = [dot(sc, v, 1, 0) + dot(qf, bef_buf[h], 1, 0) for sc, v, qf, h in zip(scs, vs_, qfs, heads)]
+        rinvs = [lax.rsqrt(jnp.mean(att * att, axis=-1, keepdims=True) + EPS) for att in atts]
+        for h, sc, att, rinv, qf in zip(heads, scs, atts, rinvs, qfs):
+            hs, vs = cols_of(h)
+            sc_buf[h] = sc
+            normed = att * rinv
+            o_ref[:, hs] = normed.astype(BF)
+            g = og_ref[:, hs].astype(F32)
+            ga = ((g - normed * jnp.mean(g * normed, axis=-1, keepdims=True)) * rinv).astype(BF)
+            ga_buf[:, hs] = ga
+            owng[h] = dot(qf, ga, 0, 0)
 
         @pl.when(z == Z - 1)
         def _():
-            bsnd[h] = og.astype(BF)
-            bcopy(h).start()
+            for h in heads:
+                bsnd[h] = owng[h].astype(BF)
+                bcopy(h).start()
 
         return 0
 
-    lax.fori_loop(0, HEADS, forward, 0)
+    lax.fori_loop(0, HEADS // PAIR, forward, 0)
 
     order = [list(range(nb)), [0] + list(range(nb - 1, 0, -1))]
 

time: 129 us -> 133 us (1.031)
  Pallas kernels: 123 us -> 126 us
    pallas_call x1, Pallas kernels: 123 us -> 126 us  [on_device(): pl.pallas_call(functools.partial(kernel, N, Z, S, scale), out_shape=(jax....]
where the time goes in v7:
time: 133 us
  Pallas kernels  126 us (95%)
  local copies, waits for them, and re-layouts  5.85 us (4%)
    pallas_call x1, Pallas kernels, on_device(): pl.pallas_call(functools.partial(kernel, N, Z, S, scale), out_shape=(jax....  126 us
    unnamed x8, local copies, waits for them, and re-layouts  5.85 us

profile of v7, /device:TPU:0, one launch (start us, length us, event | category | flops | bytes accessed | tf_op | source)
XLA Modules:
  0.0 132.9 jit_solution(4675607573967230689)
XLA Ops:
  0.6 126.4 %shard_map.75 = (bf16[256,1024]{1,0:T(8,128)(2,1)}, bf16[256,2048]{1,0:T(8,128)(2,1)}, bf16[256,1024]{1,0:T(8,128)(2,1)}, f32[64,2048]{1,0:T(8,128)}) custom-call(bf16[256,2048]{1,0:T(8,128)(2,1)} %tok.1, bf16[256,1024]{1,0:T(8,128)(2,1)} %q_ref.1, bf16[8,64,2048]{2,1,0:T(8,128)(2,1)} %bitcast.1, bf16[256,1024]{1,0:T(8,128)(2,1)} %og_ref.1), custom_call_target="tpu_custom_call" | custom-call | flops 8589934592 | bytes 4194304 | tf_op jit(solution)/shard_map/pallas_call | solution.py:419
  127.1 0.0 copy-start.1
  127.1 0.0 copy-start
  127.1 2.0 %copy.12 = bf16[256,1024]{1,0:T(8,128)(2,1)} copy(bf16[256,1024]{1,0:T(8,128)(2,1)} %get-tuple-element.8) | data formatting | bytes 1048576
  129.0 2.3 %copy.13 = bf16[256,2048]{1,0:T(8,128)(2,1)} copy(bf16[256,2048]{1,0:T(8,128)(2,1)} %get-tuple-element.9) | data formatting | bytes 2097152
  131.3 0.0 copy-done.1
  131.3 0.8 copy.14
  132.1 0.0 copy-done
  132.1 0.8 copy.15
Async XLA Ops:
  127.1 4.3 %copy-start.1 = (bf16[256,1024]{1,0:T(8,128)(2,1)S(1)}, bf16[256,1024]{1,0:T(8,128)(2,1)}, u32[]{:S(2)}) copy-start(bf16[256,1024]{1,0:T(8,128)(2,1)} %get-tuple-element.10) | copy-start | bytes 1572868
  127.1 5.1 %copy-start = (f32[64,2048]{1,0:T(8,128)S(1)}, f32[64,2048]{1,0:T(8,128)}, u32[]{:S(2)}) copy-start(f32[64,2048]{1,0:T(8,128)} %get-tuple-element.11) | copy-start | bytes 1572868
